TPU v7x, 128 devices: a whole 4x4x4 slice. The times are simulated.
128 devices in a mesh: req: 16 (over y_hi, z, core), tp: 8 (over y_lo, x).
Axes of the slice: x: 4, y: 4 (y_hi: 2, y_lo: 2; y = y_hi * 2 + y_lo), z: 4, core: 2. Of those that a mesh axis runs over, the one named last changes fastest.
Arguments:
- query: bfloat16 [512, 6, 64, 128], P('req', None, 'tp'), may hold values from -14 to 14
- k_cache: bfloat16 [512, 8, 1024, 128], P('req', 'tp'), may hold values from -14 to 14
- v_cache: bfloat16 [512, 8, 1024, 128], P('req', 'tp'), may hold values from -6 to 6
- ctx_len: int32 [512], P('req'), may hold values from 8 to 1024, as said below
- residual: bfloat16 [3072, 8192], P('req', 'tp'), may hold values from -2.5 to 2.5
- accepted: int32 [512], replicated, may hold values from 0 to 5, as said below
- w_draft: bfloat16 [8192, 8, 1024], P('tp', None, 'req'), may hold values from -0.0625 to 0.0625
Outputs:
- hidden: bfloat16 [3072, 8192], P('req', 'tp')
- grad_w: float32 [8192, 8, 1024], P('tp', None, 'req')
Inputs may be any that keep to these rules, and one draw needn't show every extreme that they name: `ctx_len`: A request's live slots end with its 6 verified positions; some request has 1024. `accepted`: the counts of each aligned block of 32 requests sum to exactly 80.
All inputs are finite; a program needn't handle non-finite values.
Results may differ from a plain program's by a relative error of at most 0.015.
Values may be sent and summed in bfloat16 or wider, within the bound.
A program may use at most 128 MiB of HBM per device.

v0:
```python
import jax
import jax.numpy as jnp
from jax import lax
from jax.sharding import PartitionSpec as P


def attend_full(grouped, k_cache, v_cache, limit, scale):
    scores = (
        jnp.einsum("rkmd,rktd->rkmt", grouped, k_cache, preferred_element_type=jnp.float32) * scale
    )
    position = jnp.arange(k_cache.shape[2], dtype=jnp.int32)
    scores = jnp.where(position < limit[..., None], scores, -jnp.inf)
    top = jnp.max(scores, axis=-1, keepdims=True)
    weights = jnp.exp(scores - top).astype(jnp.bfloat16)
    total = jnp.sum(weights.astype(jnp.float32), axis=-1, keepdims=True)
    mixed = jnp.einsum("rkmt,rktd->rkmd", weights, v_cache, preferred_element_type=jnp.float32)
    return mixed / total


def shards(query, k_cache, v_cache, ctx_len, residual, accepted, w_draft):
    requests, new_tokens, local_heads, head_dim = query.shape
    local_groups = k_cache.shape[1]
    per_group = local_heads // local_groups
    grouped = query.reshape(requests, new_tokens, local_groups, per_group, head_dim)
    grouped = grouped.transpose(0, 2, 3, 1, 4).reshape(
        requests, local_groups, per_group * new_tokens, head_dim
    )
    offsets = jnp.arange(new_tokens, dtype=jnp.int32)
    limit = ctx_len[:, None] - new_tokens + offsets[None, :] + 1
    limit = jnp.broadcast_to(limit[:, None, None, :], (requests, 1, per_group, new_tokens))
    limit = limit.reshape(requests, 1, per_group * new_tokens)
    scale = head_dim ** (-0.5)
    mixed = attend_full(grouped, k_cache, v_cache, limit, scale)
    attention = mixed.reshape(requests, local_groups, per_group, new_tokens, head_dim)
    attention = attention.transpose(0, 3, 1, 2, 4).reshape(
        requests * new_tokens, local_heads * head_dim
    )
    hidden = (residual.astype(jnp.float32) + attention).astype(jnp.bfloat16)
    feat_local = hidden.shape[1]
    group_total = w_draft.shape[1]
    slice_width = w_draft.shape[2]
    group_width = feat_local // local_groups
    req_index = lax.axis_index("req")
    w_flat = w_draft.reshape(feat_local, group_total * slice_width)
    rows_all = lax.all_gather(hidden, "req", axis=0, tiled=True)
    partial_value = jnp.dot(rows_all, w_flat, preferred_element_type=jnp.float32)
    partial_value = partial_value.reshape(rows_all.shape[0], group_total, slice_width)
    shaped_rows = rows_all.reshape(rows_all.shape[0], local_groups, group_width)
    target_rows = lax.dynamic_slice_in_dim(
        shaped_rows, req_index * slice_width, slice_width, 2
    ).astype(jnp.float32)
    summed = lax.psum_scatter(
        partial_value.astype(jnp.bfloat16), "tp", scatter_dimension=1, tiled=True
    ).astype(jnp.float32)
    total_rows = summed.shape[0]
    total_requests = total_rows // new_tokens
    shaped = target_rows.reshape(total_requests, new_tokens, local_groups, slice_width)
    following = jnp.concatenate([shaped[:, 1:], jnp.zeros_like(shaped[:, :1])], axis=1)
    following = following.reshape(total_rows, local_groups, slice_width)
    used = (offsets[None, :] < accepted[:, None]).astype(jnp.float32).reshape(total_rows, 1, 1)
    residual_grad = (used * (summed - following) / new_tokens).astype(jnp.bfloat16)
    all_grad = lax.all_gather(residual_grad, "tp", axis=1, tiled=True)
    all_grad = all_grad.reshape(total_rows, group_total * slice_width)
    contract = (((0,), (0,)), ((), ()))
    grad_w = lax.dot_general(rows_all, all_grad, contract, preferred_element_type=jnp.float32)
    return (hidden, grad_w.reshape(feat_local, group_total, slice_width))


def solution(mesh):
    placed = (
        P("req", None, "tp", None),
        P("req", "tp", None, None),
        P("req", "tp", None, None),
        P("req"),
        P("req", "tp"),
        P(),
        P("tp", None, "req"),
    )
    return jax.shard_map(
        shards,
        mesh=mesh,
        in_specs=placed,
        out_specs=(P("req", "tp"), P("tp", None, "req")),
        check_vma=False,
    )
```

profile of v0, /device:TPU:0, one launch (start us, length us, event | category | flops | bytes accessed | tf_op | source)
XLA Modules:
  0.0 200.8 jit_solution(6730633095086541307)
XLA Ops:
  7.2 0.0 copy-start
  7.2 0.0 all-gather.3.cloned.1.call-start
  7.2 0.7 broadcast_add_fusion
  8.0 0.1 copy.16
  8.1 1.1 copy.17
  9.2 0.0 slice-start
  9.2 5.7 %fusion.8 = (f32[32,48]{1,0:T(8,128)S(1)}, f32[32,48,1024]{2,1,0:T(8,128)S(1)}) fusion(s32[32,48]{1,0:T(8,128)S(1)} %copy.16, bf16[32,1,1024,128]{3,2,1,0:T(8,128)(2,1)} %param.8, bf16[32,48,128]{2,0,1:T(8,128)(2,1)S(1)} %bitcast.52), kind=kOutput, calls=%fused_computation.12 | convolution fusion | flops 408943104 | bytes 15085568 | tf_op jit(solution)/shard_map/rkmd,rktd->rkmt/dot_general | solution.py:9
  14.9 2.0 %convert_reduce_fusion = f32[32,48]{1,0:T(8,128)S(1)} fusion(f32[32,48]{1,0:T(8,128)S(1)} %get-tuple-element.2, f32[32,48,1024]{2,1,0:T(8,128)S(1)} %get-tuple-element.3, s32[32,48]{1,0:T(8,128)S(1)} %copy.16), kind=kLoop, calls=%fused_computation.8 | loop fusion | flops 11008512 | bytes 6309888 | tf_op jit(solution)/shard_map/reduce_sum | solution.py:15
  17.0 0.0 copy-start.1
  17.0 2.6 %fusion.13 = f32[32,48,128]{2,1,0:T(8,128)S(1)} fusion(bf16[32,1,1024,128]{3,2,1,0:T(8,128)(2,1)S(1)} %bitcast.54, f32[32,48]{1,0:T(8,128)S(1)} %convert_reduce_fusion, f32[32,48,1024]{2,1,0:T(8,128)S(1)} %get-tuple-element.3, f32[32,48]{1,0:T(8,128)S(1)} %get-tuple-element.2, s32[32,48]{1,0:T(8,128)S(1)} %copy.16), kind=kOutput, calls=%fused_computation.15 | convolution fusion | flops 410714112 | bytes 15484928 | tf_op jit(solution)/shard_map/rkmt,rktd->rkmd/dot_general | solution.py:16
  19.6 0.3 copy.19
  19.9 0.5 copy.20
  20.3 1.0 fusion.17
  21.3 0.0 all-gather.3.cloned.1.call-update
  21.3 0.0 reduce-scatter.2.cloned.1.call-start
  21.4 66.8 %all-gather.3.cloned.1.call-done = bf16[3072,1024]{1,0:T(8,128)(2,1)} async-done(((bf16[192,1024]{1,0:T(8,128)(2,1)}), bf16[3072,1024]{1,0:T(8,128)(2,1)}) %all-gather.3.cloned.1.call-update) | async-done | bytes 6291472 | tf_op jit(solution)/shard_map/all_gather | solution.py:45
  88.2 7.6 %fusion.9 = bf16[3072,8,64]{0,2,1:T(8,128)(2,1)} fusion(bf16[3072,1024]{1,0:T(8,128)(2,1)} %all-gather.3.cloned.1.call-done, bf16[1024,8,64]{0,2,1:T(8,128)(2,1)S(1)} %copy-done), kind=kOutput, calls=%fused_computation.13 | convolution fusion | flops 3222798336 | bytes 10485760 | tf_op jit(solution)/shard_map/dot_general | solution.py:46
  95.8 0.0 reduce-scatter.2.cloned.1.call-update
  95.9 0.2 all-gather.5.cloned.1.call-start
  96.1 0.1 fusion.19
  96.2 0.2 reshape.130
  96.4 1.4 constant_dynamic-slice_fusion
  97.8 0.3 reshape.126
  98.1 0.3 slice.5
  98.4 0.2 pad_convert_fusion
  98.7 2.7 %reshape.132 = f32[3072,1,64]{2,1,0:T(1,128)} reshape(f32[512,6,1,64]{3,1,0,2:T(8,128)S(1)} %pad_convert_fusion) | data formatting | bytes 1572864 | tf_op jit(solution)/shard_map/reshape | solution.py:59
  101.4 3.5 %copy.21 = f32[3072,1,64]{0,2,1:T(8,128)S(1)} copy(f32[3072,1,64]{2,1,0:T(1,128)} %reshape.132) | data formatting | bytes 1572864 | tf_op jit(solution)/shard_map/reshape | solution.py:59
  104.9 34.6 %reduce-scatter.2.cloned.1.call-done = bf16[3072,1,64]{0,2,1:T(8,128)(2,1)} async-done(((bf16[3072,8,64]{0,2,1:T(8,128)(2,1)}), bf16[3072,1,64]{0,2,1:T(8,128)(2,1)}) %reduce-scatter.2.cloned.1.call-update) | async-done | bytes 393232 | tf_op jit(solution)/shard_map/reduce_scatter | solution.py:52
  139.5 1.9 multiply_convert_fusion
  141.3 0.0 all-gather.5.cloned.1.call-update
  141.3 44.5 %all-gather.5.cloned.1.call-done = bf16[3072,8,64]{0,2,1:T(8,128)(2,1)} async-done(((bf16[3072,1,64]{0,2,1:T(8,128)(2,1)}), bf16[3072,8,64]{0,2,1:T(8,128)(2,1)}) %all-gather.5.cloned.1.call-update) | async-done | bytes 3145744 | tf_op jit(solution)/shard_map/all_gather | solution.py:62
  185.8 8.4 %fusion.4 = f32[1024,8,64]{0,2,1:T(8,128)} fusion(bf16[3072,1024]{1,0:T(8,128)(2,1)} %all-gather.3.cloned.1.call-done, bf16[3072,8,64]{0,2,1:T(8,128)(2,1)} %all-gather.5.cloned.1.call-done), kind=kOutput, calls=%fused_computation.4 | convolution fusion | flops 3221225472 | bytes 11534336 | tf_op jit(solution)/shard_map/dot_general | solution.py:65
  (11 shorter events, 0.0 us)
Async XLA Ops:
  7.2 81.0 %copy-start = (bf16[1024,8,64]{0,2,1:T(8,128)(2,1)S(1)}, bf16[1024,8,64]{0,2,1:T(8,128)(2,1)}, u32[]{:S(2)}) copy-start(bf16[1024,8,64]{0,2,1:T(8,128)(2,1)} %param.13) | copy-start | bytes 3145732
  7.2 81.0 %all-gather.3.cloned.1.call-start = ((), (), s32[]{:S(2)}) async-start(), calls=%async_computation.1 | async-start | bytes 6684672 | tf_op jit(solution)/shard_map/all_gather | solution.py:45
  9.2 7.8 %slice-start = ((s8[8388608]{0:T(1024)(128)(4,1)}), s8[4194304]{0:T(1024)(128)(4,1)S(1)}, s32[]{:S(2)}) async-start(s8[8388608]{0:T(1024)(128)(4,1)} %bitcast.53), calls=%async_computation.4 | async-start | bytes 8388608
  9.2 7.8 %slice-start.1 = ((s8[8388608]{0:T(1024)(128)(4,1)}), s8[4194304]{0:T(1024)(128)(4,1)S(1)}, s32[]{:S(2)}) async-start(s8[8388608]{0:T(1024)(128)(4,1)} %bitcast.53), calls=%async_computation.5 | async-start | bytes 8388608
  17.0 3.3 %copy-start.1 = (bf16[192,1024]{1,0:T(8,128)(2,1)S(1)}, bf16[192,1024]{1,0:T(8,128)(2,1)}, u32[]{:S(2)}) copy-start(bf16[192,1024]{1,0:T(8,128)(2,1)} %param.11) | copy-start | bytes 1179652
  21.3 74.8 %copy-start.2 = (s32[512]{0:T(512)S(1)}, s32[512]{0:T(512)}, u32[]{:S(2)}) copy-start(s32[512]{0:T(512)} %param.12) | copy-start | bytes 6148
  21.3 118.1 %reduce-scatter.2.cloned.1.call-start = ((), (), s32[]{:S(2)}) async-start(), calls=%async_computation.2 | async-start | bytes 3538944 | tf_op jit(solution)/shard_map/reduce_scatter | solution.py:52
  95.9 90.0 %all-gather.5.cloned.1.call-start = ((), (), s32[]{:S(2)}) async-start(), calls=%async_computation.3 | async-start | bytes 3538944 | tf_op jit(solution)/shard_map/all_gather | solution.py:62
Sparse Core Ops, SparseCore 0:
  21.4 66.7 all-gather.2
  96.0 43.4 reduce-scatter.1
  141.7 44.0 all-gather.4
where the time goes:
time: 201 us
  waiting for transfers between devices  146 us (73%)
  matrix products  24.4 us (12%)
  between operations  13.9 us (7%)
  local copies, waits for them, and re-layouts  10.3 us (5%)
  other arithmetic  5.92 us (3%)
    all_gather x1, waiting for transfers between devices, shards(): rows_all = lax.all_gather(hidden, 'req', axis=0, tiled=True)  66.8 us
    all_gather x1, waiting for transfers between devices, shards(): all_grad = lax.all_gather(residual_grad, 'tp', axis=1, tiled=True)  44.5 us
    reduce_scatter x1, waiting for transfers between devices, shards(): lax.psum_scatter(partial_value.astype(jnp.bfloat16), 'tp', scatter_dimens...  34.6 us
    dot_general x1, matrix products, shards(): lax.dot_general(rows_all, all_grad, contract, preferred_element_type=jnp....  8.43 us
    dot_general x1, matrix products, shards(): jnp.dot(rows_all, w_flat, preferred_element_type=jnp.float32)  7.64 us
    reshape x2, local copies, waits for them, and re-layouts, shards(): following = following.reshape(total_rows, local_groups, slice_width)  6.2 us
    dot_general x1, matrix products, attend_full(): jnp.einsum('rkmd,rktd->rkmt', grouped, k_cache, preferred_element_type=jn...  5.74 us
  transfers between devices with their start and end apart: 3, of which 3 were waited for; matrix products, arithmetic and copies ran while one was open for 4% of the time, Pallas kernels for 0%

commit v1 on v0

v1 whole, which is shorter than its diff:
```python
import functools

import jax
import jax.numpy as jnp
from jax import lax
from jax.experimental import pallas as pl
from jax.experimental.pallas import tpu as pltpu
from jax.sharding import PartitionSpec as P

QLEN = 6
GROUP = 8
USED_PER_BLOCK = 80
SHORT = 256
BATCH = 4

MESH = pl.DeviceIdType.MESH


def attend(queries, keys, values, length, scale):
    slots = keys.shape[0]
    scores = (
        lax.dot_general(
            queries, keys, (((1,), (1,)), ((), ())), preferred_element_type=jnp.float32
        )
        * scale
    )
    rows = queries.shape[0]
    position = lax.broadcasted_iota(jnp.int32, (rows, slots), 1)
    verified = lax.broadcasted_iota(jnp.int32, (rows, slots), 0) // GROUP
    scores = jnp.where(position < verified + (length - QLEN + 1), scores, -jnp.inf)
    top = jnp.max(scores, axis=-1, keepdims=True)
    weights = jnp.exp(scores - top).astype(jnp.bfloat16)
    total = jnp.sum(weights.astype(jnp.float32), axis=-1, keepdims=True)
    mixed = jnp.dot(weights, values, preferred_element_type=jnp.float32)
    return mixed / total


def attention_kernel(
    ctx_ref, accepted_ref, q_hbm, k_hbm, v_hbm, res_hbm,
    hidden_hbm, used_ref, foll_ref,
    q_buf, k_buf, v_buf, res_buf, att_buf, hid_buf, k_sem, v_sem, k_more, v_more, io_sem,
):
    requests, slots, head_dim = k_hbm.shape
    rows = q_buf.shape[1]
    scale = head_dim ** (-0.5)
    batches = requests // BATCH
    q_copy = pltpu.make_async_copy(q_hbm, q_buf, io_sem.at[0])
    res_copy = pltpu.make_async_copy(res_hbm, res_buf, io_sem.at[1])
    q_copy.start()

    def short_copies(b):
        span = (pl.ds(b * BATCH, BATCH), pl.ds(0, SHORT))
        return (
            pltpu.make_async_copy(k_hbm.at[span], k_buf.at[span], k_sem.at[b]),
            pltpu.make_async_copy(v_hbm.at[span], v_buf.at[span], v_sem.at[b]),
        )

    def more_copies(r):
        span = (r, pl.ds(SHORT, slots - SHORT))
        return (
            pltpu.make_async_copy(k_hbm.at[span], k_buf.at[span], k_more.at[r]),
            pltpu.make_async_copy(v_hbm.at[span], v_buf.at[span], v_more.at[r]),
        )

    for b in range(batches):
        for copy in short_copies(b):
            copy.start()
    res_copy.start()

    @pl.loop(0, requests)
    def _(r):
        @pl.when(ctx_ref[r] > SHORT)
        def _():
            for copy in more_copies(r):
                copy.start()

    q_copy.wait()

    @pl.loop(0, batches)
    def _(b):
        for copy in short_copies(b):
            copy.wait()
        for j in range(BATCH):
            r = b * BATCH + j
            att_buf[pl.ds(pl.multiple_of(r * rows, rows), rows), :] = attend(
                q_buf[r], k_buf[r, 0:SHORT], v_buf[r, 0:SHORT], ctx_ref[r], scale
            )

    @pl.loop(0, requests)
    def _(r):
        @pl.when(ctx_ref[r] > SHORT)
        def _():
            for copy in more_copies(r):
                copy.wait()
            att_buf[pl.ds(pl.multiple_of(r * rows, rows), rows), :] = attend(
                q_buf[r], k_buf[r], v_buf[r], ctx_ref[r], scale
            )

    res_copy.wait()
    all_rows = requests * QLEN
    for h in range(GROUP):
        columns = pl.ds(h * head_dim, head_dim)
        mixed = att_buf[pl.ds(h, all_rows, stride=GROUP), :]
        hid_buf[:, columns] = (res_buf[:, columns].astype(jnp.float32) + mixed).astype(jnp.bfloat16)
    hidden_copy = pltpu.make_async_copy(hid_buf, hidden_hbm, io_sem.at[2])
    hidden_copy.start()

    row = lax.broadcasted_iota(jnp.int32, (1, all_rows), 1)
    request = row // QLEN
    verified = row - request * QLEN
    base = lax.axis_index("req") * requests
    place = jnp.full((1, all_rows), -1, jnp.int32)
    next_place = place
    before = jnp.int32(0)
    for r in range(requests):
        count = accepted_ref[base + r]
        mine = request == r
        place = jnp.where(mine & (verified < count), before + verified, place)
        next_place = jnp.where(
            mine & (verified >= 1) & (verified <= count), before + verified - 1, next_place
        )
        before = before + count
    hidden = hid_buf[...]
    want = lax.broadcasted_iota(jnp.int32, (used_ref.shape[0], all_rows), 0)
    pick = (want == place).astype(jnp.float32).astype(jnp.bfloat16)
    used_ref[...] = jnp.dot(pick, hidden, preferred_element_type=jnp.float32).astype(jnp.bfloat16)
    want = lax.broadcasted_iota(jnp.int32, (foll_ref.shape[1], all_rows), 0)
    pick = (want == next_place).astype(jnp.float32).astype(jnp.bfloat16)
    following = jnp.dot(pick, hidden, preferred_element_type=jnp.float32)
    foll_ref[...] = following.T.astype(jnp.bfloat16)
    hidden_copy.wait()


def attention(query, k_cache, v_cache, ctx_len, residual, accepted):
    requests, slots, head_dim = k_cache.shape
    rows = query.shape[1]
    all_rows, features = residual.shape
    any_spec = pl.BlockSpec(memory_space=pl.ANY)
    smem = pl.BlockSpec(memory_space=pltpu.SMEM)
    vmem = pl.BlockSpec(memory_space=pltpu.VMEM)
    batches = requests // BATCH
    return pl.pallas_call(
        attention_kernel,
        out_shape=(
            jax.ShapeDtypeStruct((all_rows, features), jnp.bfloat16),
            jax.ShapeDtypeStruct((USED_PER_BLOCK, features), jnp.bfloat16),
            jax.ShapeDtypeStruct((features, 128), jnp.bfloat16),
        ),
        in_specs=[smem, smem, any_spec, any_spec, any_spec, any_spec],
        out_specs=(any_spec, vmem, vmem),
        scratch_shapes=[
            pltpu.VMEM((requests, rows, head_dim), jnp.bfloat16),
            pltpu.VMEM((requests, slots, head_dim), jnp.bfloat16),
            pltpu.VMEM((requests, slots, head_dim), jnp.bfloat16),
            pltpu.VMEM((all_rows, features), jnp.bfloat16),
            pltpu.VMEM((requests * rows, head_dim), jnp.float32),
            pltpu.VMEM((all_rows, features), jnp.bfloat16),
            pltpu.SemaphoreType.DMA((batches,)),
            pltpu.SemaphoreType.DMA((batches,)),
            pltpu.SemaphoreType.DMA((requests,)),
            pltpu.SemaphoreType.DMA((requests,)),
            pltpu.SemaphoreType.DMA((3,)),
        ],
        compiler_params=pltpu.CompilerParams(vmem_limit_bytes=40 * 2**20),
        name="attention",
    )(ctx_len, accepted, query, k_cache, v_cache, residual)


OFFSETS = ((0, 0), (0, 1), (0, 3), (0, 2), (1, 0), (1, 1), (1, 3), (1, 2))


def gradient_kernel(
    n_tp, used_ref, foll_ref, w_ref, out_ref,
    hid, w_buf, foll, place, part, sums, grad, total,
    io_sem, ag_send, ag_recv, sib_send, sib_recv, fo_send, fo_recv,
    rs_send, rs_recv, gg_send, gg_recv,
):
    r = lax.axis_index("req")
    t = lax.axis_index("tp")
    core = lax.rem(r, 2)
    z = lax.rem(r // 2, 4)
    y_hi = r // 8
    sibling = r + 1 - 2 * core
    n_req = 16
    block = used_ref.shape[0]
    width = foll.shape[1]
    chunk = part.shape[2]

    def rows_of(source):
        return pl.ds(pl.multiple_of(source * block, block), block)

    w_copy = pltpu.make_async_copy(w_ref, w_buf, io_sem.at[0])
    own_copy = pltpu.make_async_copy(used_ref, hid.at[rows_of(r)], io_sem.at[1])
    foll_copy = pltpu.make_async_copy(
        foll_ref.at[pl.ds(pl.multiple_of(r * width, width), width)], foll.at[r], io_sem.at[2]
    )
    w_copy.start()
    own_copy.start()
    foll_copy.start()

    barrier = pltpu.get_barrier_semaphore()

    @pl.loop(1, n_req)
    def _(i):
        pl.semaphore_signal(
            barrier, inc=1, device_id={"req": lax.rem(r + i, n_req)}, device_id_type=MESH
        )

    @pl.loop(1, n_tp)
    def _(i):
        pl.semaphore_signal(
            barrier, inc=1, device_id={"tp": lax.rem(t + i, n_tp)}, device_id_type=MESH
        )

    pl.semaphore_wait(barrier, n_req - 1 + n_tp - 1)

    def peer(k, sign):
        dy, dz = OFFSETS[k]
        return (lax.rem(y_hi + dy, 2) * 4 + lax.rem(z + 4 + sign * dz, 4)) * 2 + core

    def gather_copy(k):
        return pltpu.make_async_remote_copy(
            src_ref=used_ref, dst_ref=hid.at[rows_of(r)],
            send_sem=ag_send.at[k], recv_sem=ag_recv.at[k],
            device_id={"req": peer(k, 1)}, device_id_type=MESH,
        )

    def sibling_copy(k):
        source = peer(k, -1)
        return pltpu.make_async_remote_copy(
            src_ref=used_ref if k == 0 else hid.at[rows_of(source)],
            dst_ref=hid.at[rows_of(source)],
            send_sem=sib_send.at[k], recv_sem=sib_recv.at[k],
            device_id={"req": sibling}, device_id_type=MESH,
        )

    def gather_wait(k):
        pltpu.make_async_remote_copy(
            src_ref=used_ref, dst_ref=hid.at[rows_of(peer(k, -1))],
            send_sem=ag_send.at[k], recv_sem=ag_recv.at[k],
            device_id={"req": peer(k, 1)}, device_id_type=MESH,
        ).wait_recv()

    def sibling_wait(k):
        source = peer(k, -1)
        other = source + 1 - 2 * core
        pltpu.make_async_remote_copy(
            src_ref=used_ref, dst_ref=hid.at[rows_of(other)],
            send_sem=sib_send.at[k], recv_sem=sib_recv.at[k],
            device_id={"req": sibling}, device_id_type=MESH,
        ).wait_recv()

    sibling_copy(0).start()
    for k in range(1, 8):
        gather_copy(k).start()

    def foll_exchange(i):
        target = lax.rem(r + i, n_req)
        return pltpu.make_async_remote_copy(
            src_ref=foll_ref.at[pl.ds(pl.multiple_of(target * width, width), width)],
            dst_ref=foll.at[r],
            send_sem=fo_send.at[i], recv_sem=fo_recv.at[i],
            device_id={"req": target}, device_id_type=MESH,
        )

    @pl.loop(1, n_req)
    def _(i):
        foll_exchange(i).start()

    @pl.loop(0, 8)
    def _(s):
        j = lax.broadcasted_iota(jnp.int32, (128, chunk), 0)
        column = lax.broadcasted_iota(jnp.int32, (128, chunk), 1)
        hit = (column == s * block + j) & (j < block)
        place[pl.ds(pl.multiple_of(s * 128, 128), 128), :] = hit.astype(jnp.float32).astype(
            jnp.bfloat16
        )

    own_copy.wait()
    w_copy.wait()

    def rs_copy(h, i):
        target = lax.rem(t + i, n_tp)
        return pltpu.make_async_remote_copy(
            src_ref=part.at[h, pl.ds(pl.multiple_of(target * width, width), width)],
            dst_ref=sums.at[h, i],
            send_sem=rs_send.at[h, i], recv_sem=rs_recv.at[h, i],
            device_id={"tp": target}, device_id_type=MESH,
        )

    def gg_copy(h, i):
        mine = pl.ds(pl.multiple_of(t * width, width), width)
        return pltpu.make_async_remote_copy(
            src_ref=grad.at[h, mine], dst_ref=grad.at[h, mine],
            send_sem=gg_send.at[h, i], recv_sem=gg_recv.at[h, i],
            device_id={"tp": lax.rem(t + i, n_tp)}, device_id_type=MESH,
        )

    def gg_wait(h, i):
        source = lax.rem(t + n_tp - i, n_tp)
        theirs = pl.ds(pl.multiple_of(source * width, width), width)
        pltpu.make_async_remote_copy(
            src_ref=grad.at[h, theirs], dst_ref=grad.at[h, theirs],
            send_sem=gg_send.at[h, i], recv_sem=gg_recv.at[h, i],
            device_id={"tp": lax.rem(t + i, n_tp)}, device_id_type=MESH,
        ).wait_recv()

    def chunk_start(h):
        return pl.multiple_of(lax.rem(y_hi + h, 2) * chunk, chunk)

    def draft(h):
        start = chunk_start(h)

        @pl.loop(0, chunk // 128)
        def _(n):
            rows = hid[pl.ds(pl.multiple_of(start + n * 128, 128), 128), :]
            part[h, :, pl.ds(pl.multiple_of(n * 128, 128), 128)] = lax.dot_general(
                w_buf[...], rows, (((1,), (1,)), ((), ())), preferred_element_type=jnp.float32
            ).astype(jnp.bfloat16)

        @pl.loop(1, n_tp)
        def _(i):
            rs_copy(h, i).start()

    def loss_grad(h):
        @pl.loop(1, n_tp)
        def _(i):
            rs_copy(h, i).wait_recv()

        mine = pl.ds(pl.multiple_of(t * width, width), width)
        summed = part[h, mine, :].astype(jnp.float32)
        for i in range(1, n_tp):
            summed = summed + sums[h, i].astype(jnp.float32)
        first = lax.rem(y_hi + h, 2) * 8
        rows = jnp.concatenate([foll[first + s] for s in range(8)], axis=1)
        following = jnp.dot(rows, place[...], preferred_element_type=jnp.float32)
        grad[h, mine, :] = ((summed - following) / QLEN).astype(jnp.bfloat16)

        @pl.loop(1, n_tp)
        def _(i):
            gg_copy(h, i).start()

    def project(h):
        @pl.loop(1, n_tp)
        def _(i):
            gg_wait(h, i)

        start = chunk_start(h)
        features = hid.shape[1]
        tile = min(256, features)

        @pl.loop(0, features // tile)
        def _(n):
            columns = pl.ds(pl.multiple_of(n * tile, tile), tile)
            value = jnp.dot(
                grad[h], hid[pl.ds(start, chunk), columns], preferred_element_type=jnp.float32
            )
            if h == 0:
                total[:, columns] = value
            else:
                total[:, columns] += value

    for h in range(2):
        for k in range(4 * h, 4 * h + 4):
            if k > 0:
                gather_wait(k)
                sibling_copy(k).start()
        for k in range(4 * h, 4 * h + 4):
            sibling_wait(k)
        draft(h)

    @pl.loop(1, n_req)
    def _(i):
        source = lax.rem(r + n_req - i, n_req)
        pltpu.make_async_remote_copy(
            src_ref=foll.at[source], dst_ref=foll.at[source],
            send_sem=fo_send.at[i], recv_sem=fo_recv.at[i],
            device_id={"req": source}, device_id_type=MESH,
        ).wait_recv()

    foll_copy.wait()
    for h in range(2):
        loss_grad(h)
    for h in range(2):
        project(h)
    out_copy = pltpu.make_async_copy(total, out_ref, io_sem.at[3])
    out_copy.start()

    sibling_copy(0).wait_send()
    for k in range(1, 8):
        gather_copy(k).wait_send()
        sibling_copy(k).wait_send()

    @pl.loop(1, n_req)
    def _(i):
        foll_exchange(i).wait_send()

    for h in range(2):

        @pl.loop(1, n_tp)
        def _(i):
            rs_copy(h, i).wait_send()
            gg_copy(h, i).wait_send()

    out_copy.wait()


def gradient(used, foll, w_flat, n_tp):
    block, features = used.shape
    outs = w_flat.shape[0]
    width = outs // n_tp
    chunk = 8 * block
    any_spec = pl.BlockSpec(memory_space=pl.ANY)
    dma = pltpu.SemaphoreType.DMA
    return pl.pallas_call(
        functools.partial(gradient_kernel, n_tp),
        out_shape=jax.ShapeDtypeStruct((outs, features), jnp.float32),
        in_specs=[any_spec] * 3,
        out_specs=any_spec,
        scratch_shapes=[
            pltpu.VMEM((2 * chunk, features), jnp.bfloat16),
            pltpu.VMEM((outs, features), jnp.bfloat16),
            pltpu.VMEM((16, width, 128), jnp.bfloat16),
            pltpu.VMEM((8 * 128, chunk), jnp.bfloat16),
            pltpu.VMEM((2, outs, chunk), jnp.bfloat16),
            pltpu.VMEM((2, n_tp, width, chunk), jnp.bfloat16),
            pltpu.VMEM((2, outs, chunk), jnp.bfloat16),
            pltpu.VMEM((outs, features), jnp.float32),
            dma((4,)), dma((8,)), dma((8,)), dma((8,)), dma((8,)), dma((16,)), dma((16,)),
            dma((2, n_tp)), dma((2, n_tp)), dma((2, n_tp)), dma((2, n_tp)),
        ],
        compiler_params=pltpu.CompilerParams(
            collective_id=0, has_side_effects=True, vmem_limit_bytes=40 * 2**20
        ),
        name="gradient",
    )(used, foll, w_flat)


def shards(query, k_cache, v_cache, ctx_len, residual, accepted, w_draft):
    requests, new_tokens, heads, head_dim = query.shape
    slots = k_cache.shape[2]
    hidden, used, foll = attention(
        query.reshape(requests, new_tokens * heads, head_dim),
        k_cache.reshape(requests, slots, head_dim),
        v_cache.reshape(requests, slots, head_dim),
        ctx_len, residual, accepted,
    )
    features, groups, width = w_draft.shape
    w_flat = w_draft.transpose(1, 2, 0).reshape(groups * width, features)
    grad = gradient(used, foll, w_flat, groups)
    return hidden, grad.reshape(groups, width, features).transpose(2, 0, 1)


def solution(mesh):
    placed = (
        P("req", None, "tp", None),
        P("req", "tp", None, None),
        P("req", "tp", None, None),
        P("req"),
        P("req", "tp"),
        P(),
        P("tp", None, "req"),
    )
    return jax.shard_map(
        shards,
        mesh=mesh,
        in_specs=placed,
        out_specs=(P("req", "tp"), P("tp", None, "req")),
        check_vma=False,
    )
```

time: 201 us -> 85.9 us (0.43)
  waiting for transfers between devices: 146 us -> 0 us
  Pallas kernels: 0 us -> 75.6 us
  matrix products: 24.4 us -> 0 us
  between operations: 13.9 us -> 0.67 us
  other arithmetic: 5.92 us -> 0 us
  local copies, waits for them, and re-layouts: 10.3 us -> 8.03 us
    all_gather x2 -> x0, waiting for transfers between devices: 111 us -> none  [the longest x1 66.8 us: shards(): rows_all = lax.all_gather(hidden, 'req', axis=0, tiled=True)]
    pallas_call x0 -> x2, Pallas kernels: none -> 75.6 us  [the longest x1 62.9 us: gradient(): pl.pallas_call(functools.partial(gradient_kernel, n_tp), out_shape=jax.Sh...]
    reduce_scatter x1 -> x0, waiting for transfers between devices: 34.6 us -> none  [shards(): lax.psum_scatter(partial_value.astype(jnp.bfloat16), 'tp', scatter_dimens...]
    dot_general x4 -> x0, matrix products: 24.4 us -> none  [the longest x1 8.43 us: shards(): lax.dot_general(rows_all, all_grad, contract, preferred_element_type=jnp....]
    unnamed x11 -> x13, local copies, waits for them, and re-layouts: 1.14 us -> 8.03 us
    reshape x3 -> x0, local copies, waits for them, and re-layouts: 6.51 us -> none  [the longest x2 6.2 us: shards(): following = following.reshape(total_rows, local_groups, slice_width)]
    convert_element_type x3 -> x0, other arithmetic: 2.95 us -> none  [the longest x1 1.86 us: shards(): (used * (summed - following) / new_tokens).astype(jnp.bfloat16)]
    reduce_sum x1 -> x0, other arithmetic: 2.02 us -> none  [attend_full(): total = jnp.sum(weights.astype(jnp.float32), axis=-1, keepdims=True)]
  transfers between devices with their start and end apart: 3 -> 0, of which waited for: 3 -> 0; matrix products, arithmetic and copies ran while one was open for 4% -> 0% of each run, Pallas kernels for 0% -> 0%
where the time goes in v1:
time: 85.9 us; the launch traced here: 84.3 us
  Pallas kernels  75.6 us (88%)
  local copies, waits for them, and re-layouts  8.03 us (9%)
    pallas_call x1, Pallas kernels, gradient(): pl.pallas_call(functools.partial(gradient_kernel, n_tp), out_shape=jax.Sh...  62.9 us
    pallas_call x1, Pallas kernels, attention(): pl.pallas_call(attention_kernel, out_shape=(jax.ShapeDtypeStruct((all_row...  12.7 us
    unnamed x13, local copies, waits for them, and re-layouts  8.03 us

profile of v1, /device:TPU:0, one launch (start us, length us, event | category | flops | bytes accessed | tf_op | source)
XLA Modules:
  0.0 84.3 jit_solution(14270223959910726724)
XLA Ops:
  0.6 0.0 copy-start
  0.6 3.4 %copy-done = bf16[32,1,1024,128]{3,2,1,0:T(8,128)(2,1)S(1)} copy-done((bf16[32,1,1024,128]{3,2,1,0:T(8,128)(2,1)S(1)}, bf16[32,1,1024,128]{3,2,1,0:T(8,128)(2,1)}, u32[]{:S(2)}) %copy-start) | copy-done | bytes 8388632
  4.0 0.0 copy-start.2
  4.0 1.0 %copy-done.2 = bf16[32,6,8,128]{3,2,1,0:T(8,128)(2,1)S(1)} copy-done((bf16[32,6,8,128]{3,2,1,0:T(8,128)(2,1)S(1)}, bf16[32,6,8,128]{3,2,1,0:T(8,128)(2,1)}, u32[]{:S(2)}) %copy-start.2) | copy-done | bytes 393240
  5.0 0.0 copy-start.3
  5.0 1.0 %copy-done.3 = bf16[192,1024]{1,0:T(8,128)(2,1)S(1)} copy-done((bf16[192,1024]{1,0:T(8,128)(2,1)S(1)}, bf16[192,1024]{1,0:T(8,128)(2,1)}, u32[]{:S(2)}) %copy-start.3) | copy-done | bytes 393240
  6.0 0.0 copy-start.4
  6.0 0.7 copy-done.4
  6.7 0.0 copy-start.5
  6.7 0.7 copy-done.5
  7.3 0.0 copy-start.1
  7.3 12.7 %attention.1 = (bf16[192,1024]{1,0:T(8,128)(2,1)}, bf16[80,1024]{1,0:T(8,128)(2,1)S(1)}, bf16[1024,128]{1,0:T(8,128)(2,1)S(1)}) custom-call(s32[32]{0:T(128)S(1)} %copy-done.5, s32[512]{0:T(512)S(1)} %copy-done.4, bf16[32,48,128]{2,1,0:T(8,128)(2,1)S(1)} %bitcast.12, bf16[32,1024,128]{2,1,0:T(8,128)(2,1)S(1)} %bitcast.10, bf16[32,1024,128]{2,1,0:T(8,128)(2,1)} %bitcast.13, ...), custom_call_target="tpu_custom_call" | custom-call | tf_op jit(solution)/shard_map/attention/pallas_call | solution.py:142
  20.0 0.0 copy-done.1
  20.0 62.9 %gradient.1 = f32[512,1024]{1,0:T(8,128)S(1)} custom-call(bf16[80,1024]{1,0:T(8,128)(2,1)S(1)} %get-tuple-element.6.used_ref, bf16[1024,128]{1,0:T(8,128)(2,1)S(1)} %get-tuple-element.7.foll_ref, bf16[512,1024]{1,0:T(8,128)(2,1)S(1)} %bitcast.11), custom_call_target="tpu_custom_call" | custom-call | tf_op jit(solution)/shard_map/gradient/pallas_call | solution.py:415
  82.9 1.3 %copy.10 = f32[1024,8,64]{0,2,1:T(8,128)} copy(f32[1024,8,64]{0,2,1:T(8,128)S(1)} %bitcast.9) | data formatting | bytes 4194304
Async XLA Ops:
  0.6 3.4 %copy-start = (bf16[32,1,1024,128]{3,2,1,0:T(8,128)(2,1)S(1)}, bf16[32,1,1024,128]{3,2,1,0:T(8,128)(2,1)}, u32[]{:S(2)}) copy-start(bf16[32,1,1024,128]{3,2,1,0:T(8,128)(2,1)} %param.8) | copy-start | bytes 25165828
  4.0 1.0 %copy-start.2 = (bf16[32,6,8,128]{3,2,1,0:T(8,128)(2,1)S(1)}, bf16[32,6,8,128]{3,2,1,0:T(8,128)(2,1)}, u32[]{:S(2)}) copy-start(bf16[32,6,8,128]{3,2,1,0:T(8,128)(2,1)} %param.7) | copy-start | bytes 1179652
  5.0 1.0 %copy-start.3 = (bf16[192,1024]{1,0:T(8,128)(2,1)S(1)}, bf16[192,1024]{1,0:T(8,128)(2,1)}, u32[]{:S(2)}) copy-start(bf16[192,1024]{1,0:T(8,128)(2,1)} %res_hbm.1) | copy-start | bytes 1179652
  6.0 0.7 copy-start.4
  6.7 0.7 copy-start.5
  7.3 12.7 %copy-start.1 = (bf16[1024,8,64]{0,2,1:T(8,128)(2,1)S(1)}, bf16[1024,8,64]{0,2,1:T(8,128)(2,1)}, u32[]{:S(2)}) copy-start(bf16[1024,8,64]{0,2,1:T(8,128)(2,1)} %param.13) | copy-start | bytes 3145732

commit v2 on v1

v2 whole, which is shorter than its diff:
```python
import jax
import jax.numpy as jnp
from jax import lax
from jax.experimental import pallas as pl
from jax.experimental.pallas import tpu as pltpu
from jax.sharding import PartitionSpec as P

QLEN = 6
LOG2_E = 1.4426950408889634
GROUP = 8
USED_PER_BLOCK = 80
SHORT = 256
BATCH = 16

MESH = pl.DeviceIdType.MESH


def attend(queries, keys, values, length, scale):
    slots = keys.shape[0]
    scores = lax.dot_general(
        queries, keys, (((1,), (1,)), ((), ())), preferred_element_type=jnp.float32
    ) * (scale * LOG2_E)
    rows, features = queries.shape
    position = lax.broadcasted_iota(jnp.int32, (rows, slots), 1)
    verified = lax.broadcasted_iota(jnp.int32, (rows, slots), 0) // GROUP
    scores = jnp.where(position < verified + (length - QLEN + 1), scores, -jnp.inf)
    top = jnp.max(scores, axis=-1, keepdims=True)
    weights = jnp.exp2(scores - top).astype(jnp.bfloat16)
    values = jnp.concatenate([values, jnp.ones((slots, features), jnp.bfloat16)], axis=1)
    mixed = jnp.dot(weights, values, preferred_element_type=jnp.float32)
    return mixed[:, :features] / mixed[:, features:]


def attention_kernel(
    ctx_ref, accepted_ref, q_hbm, k_hbm, v_hbm, res_hbm,
    hidden_hbm, used_ref, foll_ref,
    q_buf, k_buf, v_buf, res_buf, att_buf, hid_buf, k_sem, v_sem, k_more, v_more, io_sem,
):
    requests, slots, head_dim = k_hbm.shape
    rows = q_buf.shape[1]
    scale = head_dim ** (-0.5)
    batches = requests // BATCH
    q_copy = pltpu.make_async_copy(q_hbm, q_buf, io_sem.at[0])
    res_copy = pltpu.make_async_copy(res_hbm, res_buf, io_sem.at[1])
    q_copy.start()

    def short_copies(b):
        span = (pl.ds(b * BATCH, BATCH), pl.ds(0, SHORT))
        return (
            pltpu.make_async_copy(k_hbm.at[span], k_buf.at[span], k_sem.at[b]),
            pltpu.make_async_copy(v_hbm.at[span], v_buf.at[span], v_sem.at[b]),
        )

    def more_copies(r):
        span = (r, pl.ds(SHORT, slots - SHORT))
        return (
            pltpu.make_async_copy(k_hbm.at[span], k_buf.at[span], k_more.at[r]),
            pltpu.make_async_copy(v_hbm.at[span], v_buf.at[span], v_more.at[r]),
        )

    for b in range(batches):
        for copy in short_copies(b):
            copy.start()
    res_copy.start()

    @pl.loop(0, requests)
    def _(r):
        @pl.when(ctx_ref[r] > SHORT)
        def _():
            for copy in more_copies(r):
                copy.start()

    q_copy.wait()

    @pl.loop(0, batches)
    def _(b):
        for copy in short_copies(b):
            copy.wait()
        for j in range(BATCH):
            r = b * BATCH + j
            att_buf[pl.ds(pl.multiple_of(r * rows, rows), rows), :] = attend(
                q_buf[r], k_buf[r, 0:SHORT], v_buf[r, 0:SHORT], ctx_ref[r], scale
            )

    @pl.loop(0, requests)
    def _(r):
        @pl.when(ctx_ref[r] > SHORT)
        def _():
            for copy in more_copies(r):
                copy.wait()
            att_buf[pl.ds(pl.multiple_of(r * rows, rows), rows), :] = attend(
                q_buf[r], k_buf[r], v_buf[r], ctx_ref[r], scale
            )

    res_copy.wait()
    all_rows = requests * QLEN
    for h in range(GROUP):
        columns = pl.ds(h * head_dim, head_dim)
        mixed = att_buf[pl.ds(h, all_rows, stride=GROUP), :]
        hid_buf[:, columns] = (res_buf[:, columns].astype(jnp.float32) + mixed).astype(jnp.bfloat16)
    hidden_copy = pltpu.make_async_copy(hid_buf, hidden_hbm, io_sem.at[2])
    hidden_copy.start()

    row = lax.broadcasted_iota(jnp.int32, (1, all_rows), 1)
    request = row // QLEN
    verified = row - request * QLEN
    base = lax.axis_index("req") * requests
    place = jnp.full((1, all_rows), -1, jnp.int32)
    next_place = place
    before = jnp.int32(0)
    for r in range(requests):
        count = accepted_ref[base + r]
        mine = request == r
        place = jnp.where(mine & (verified < count), before + verified, place)
        next_place = jnp.where(
            mine & (verified >= 1) & (verified <= count), before + verified - 1, next_place
        )
        before = before + count
    hidden = hid_buf[...]
    want = lax.broadcasted_iota(jnp.int32, (used_ref.shape[0], all_rows), 0)
    pick = (want == place).astype(jnp.float32).astype(jnp.bfloat16)
    used_ref[...] = jnp.dot(pick, hidden, preferred_element_type=jnp.float32).astype(jnp.bfloat16)
    want = lax.broadcasted_iota(jnp.int32, (foll_ref.shape[1], all_rows), 0)
    pick = (want == next_place).astype(jnp.float32).astype(jnp.bfloat16)
    following = jnp.dot(pick, hidden, preferred_element_type=jnp.float32)
    foll_ref[...] = following.T.astype(jnp.bfloat16)
    hidden_copy.wait()


def attention(query, k_cache, v_cache, ctx_len, residual, accepted):
    requests, slots, head_dim = k_cache.shape
    rows = query.shape[1]
    all_rows, features = residual.shape
    any_spec = pl.BlockSpec(memory_space=pl.ANY)
    smem = pl.BlockSpec(memory_space=pltpu.SMEM)
    vmem = pl.BlockSpec(memory_space=pltpu.VMEM)
    batches = requests // BATCH
    return pl.pallas_call(
        attention_kernel,
        out_shape=(
            jax.ShapeDtypeStruct((all_rows, features), jnp.bfloat16),
            jax.ShapeDtypeStruct((USED_PER_BLOCK, features), jnp.bfloat16),
            jax.ShapeDtypeStruct((features, 128), jnp.bfloat16),
        ),
        in_specs=[smem, smem, any_spec, any_spec, any_spec, any_spec],
        out_specs=(any_spec, vmem, vmem),
        scratch_shapes=[
            pltpu.VMEM((requests, rows, head_dim), jnp.bfloat16),
            pltpu.VMEM((requests, slots, head_dim), jnp.bfloat16),
            pltpu.VMEM((requests, slots, head_dim), jnp.bfloat16),
            pltpu.VMEM((all_rows, features), jnp.bfloat16),
            pltpu.VMEM((requests * rows, head_dim), jnp.float32),
            pltpu.VMEM((all_rows, features), jnp.bfloat16),
            pltpu.SemaphoreType.DMA((batches,)),
            pltpu.SemaphoreType.DMA((batches,)),
            pltpu.SemaphoreType.DMA((requests,)),
            pltpu.SemaphoreType.DMA((requests,)),
            pltpu.SemaphoreType.DMA((3,)),
        ],
        compiler_params=pltpu.CompilerParams(vmem_limit_bytes=60 * 2**20),
        name="attention",
    )(ctx_len, accepted, query, k_cache, v_cache, residual)


SOURCES = ((0, 0), (0, 1), (0, 3), (0, 2), (1, 0), (1, 1), (1, 3), (1, 2))
PIECES = ((0, 48), (48, 32))
CHUNKS = (
    ((0, 1, 2, 3), ((0, 384, "x"), (384, 256, "y"))),
    ((4, 5, 6), ((640, 256, "x"), (896, 128, "y"))),
    ((7,), ((1024, 128, "x"), (1152, 128, "y"))),
)
PARTS = tuple(part for _, parts in CHUNKS for part in parts)


def gradient_kernel(
    used_ref, foll_ref, w_ref, out_ref,
    hid, w_buf, foll, place, following, part, first_x, first_y, half, own, second, grad, total,
    io_sem, g_send, g_recv, sib_send, sib_recv, fo_send, fo_recv,
    s1_send, s1_recv, s2_send, s2_recv, a1_send, a1_recv, a2_send, a2_recv,
):
    r = lax.axis_index("req")
    t = lax.axis_index("tp")
    core = lax.rem(r, 2)
    z = lax.rem(r // 2, 4)
    y_hi = r // 8
    x = lax.rem(t, 4)
    y_lo = t // 4
    other = 1 - y_lo
    block, features = used_ref.shape
    width = foll.shape[1]
    rows_all = hid.shape[0]

    def req_at(dy, dz, dc):
        return (lax.rem(y_hi + dy, 2) * 4 + lax.rem(z + 4 + dz, 4)) * 2 + lax.rem(core + dc, 2)

    def tp_x(i):
        return {"tp": y_lo * 4 + lax.rem(x + i, 4)}

    tp_y = {"tp": other * 4 + x}

    def remote(src, dst, send, recv, device):
        return pltpu.make_async_remote_copy(
            src_ref=src, dst_ref=dst, send_sem=send, recv_sem=recv,
            device_id=device, device_id_type=MESH,
        )

    w_copy = pltpu.make_async_copy(w_ref, w_buf, io_sem.at[0])
    own_copy = pltpu.make_async_copy(used_ref, hid.at[pl.ds(0, block)], io_sem.at[1])
    foll_copy = pltpu.make_async_copy(
        foll_ref.at[pl.ds(pl.multiple_of(r * width, width), width)], foll.at[0], io_sem.at[2]
    )
    own_copy.start()
    w_copy.start()
    foll_copy.start()

    barrier = pltpu.get_barrier_semaphore()
    for dy, dz in SOURCES:
        for dc in range(2):
            if (dy, dz, dc) != (0, 0, 0):
                pl.semaphore_signal(
                    barrier, inc=1, device_id={"req": req_at(dy, dz, dc)}, device_id_type=MESH
                )
    for i in range(1, 4):
        pl.semaphore_signal(barrier, inc=1, device_id=tp_x(i), device_id_type=MESH)
    pl.semaphore_signal(barrier, inc=1, device_id=tp_y, device_id_type=MESH)
    pl.semaphore_wait(barrier, 19)

    def shard(k, p):
        start, rows = PIECES[p]
        return hid.at[pl.ds(2 * block * k + start, rows)]

    def gather(k, p):
        start, rows = PIECES[p]
        mine = used_ref.at[pl.ds(start, rows)]
        if k == 1:
            src, target = mine, (0, -1)
        elif k == 2:
            src, target = mine, (0, 1)
        elif k == 3:
            src, target = (shard(2, 0), (0, 1)) if p == 0 else (shard(1, 1), (0, -1))
        elif k == 4:
            src, target = mine, (1, 0)
        elif k == 5:
            src, target = shard(4, p), (0, -1)
        elif k == 6:
            src, target = shard(4, p), (0, 1)
        else:
            src, target = (shard(6, 0), (0, 1)) if p == 0 else (shard(5, 1), (0, -1))
        return remote(
            src, shard(k, p), g_send.at[k, p], g_recv.at[k, p], {"req": req_at(*target, 0)}
        )

    def sibling(k):
        src = used_ref if k == 0 else hid.at[pl.ds(2 * block * k, block)]
        dst = hid.at[pl.ds(2 * block * k + block, block)]
        return remote(src, dst, sib_send.at[k], sib_recv.at[k], {"req": req_at(0, 0, 1)})

    for p in range(2):
        gather(2, p).start()
        gather(1, 1 - p).start()
        gather(4, p).start()
    sibling(0).start()

    half_rows = rows_all // 2

    @pl.loop(0, 8)
    def _(s):
        j = lax.broadcasted_iota(jnp.int32, (128, half_rows), 0)
        column = lax.broadcasted_iota(jnp.int32, (128, half_rows), 1)
        hit = (column == s * block + j) & (j < block)
        place[pl.ds(pl.multiple_of(s * 128, 128), 128), :] = hit.astype(jnp.float32).astype(
            jnp.bfloat16
        )

    own_copy.wait()
    w_copy.wait()

    def foll_exchange(k, dc):
        dy, dz = SOURCES[k]
        target = req_at(dy, -dz, dc)
        src = foll_ref.at[pl.ds(pl.multiple_of(target * width, width), width)]
        j = 2 * k + dc
        return remote(src, foll.at[j], fo_send.at[j], fo_recv.at[j], {"req": target})

    foll_peers = [(k, dc) for k in range(8) for dc in range(2) if (k, dc) != (0, 0)]

    def lanes(f):
        return pl.ds(PARTS[f][0], PARTS[f][1])

    def sum_first(f, i):
        if i:
            src = part.at[:, lax.rem(x + i, 4), :, lanes(f)]
            return remote(
                src, first_x.at[i - 1, :, :, lanes(f)], s1_send.at[f, i], s1_recv.at[f, i], tp_x(i)
            )
        src = part.at[other, :, :, lanes(f)]
        return remote(src, first_y.at[:, :, lanes(f)], s1_send.at[f, 0], s1_recv.at[f, 0], tp_y)

    def sum_second(f, i):
        slot = (i - 1) % 4
        src, dst = half.at[slot, :, lanes(f)], second.at[slot, :, lanes(f)]
        device = tp_x(i) if i else tp_y
        return remote(src, dst, s2_send.at[f, i], s2_recv.at[f, i], device)

    def grad_first(f, i):
        mine = grad.at[y_lo, x, :, lanes(f)]
        return remote(mine, mine, a1_send.at[f, i], a1_recv.at[f, i], tp_x(i) if i else tp_y)

    def grad_first_wait(f, i):
        theirs = grad.at[y_lo, lax.rem(x + 4 - i, 4), :, lanes(f)] if i else grad.at[
            other, x, :, lanes(f)
        ]
        remote(
            theirs, theirs, a1_send.at[f, i], a1_recv.at[f, i], tp_x(i) if i else tp_y
        ).wait_recv()

    def grad_second(f, i):
        if PARTS[f][2] == "x":
            mine, device = grad.at[other, x, :, lanes(f)], tp_x(i)
        else:
            mine, device = grad.at[y_lo, lax.rem(x + 4 - i, 4), :, lanes(f)], tp_y
        return remote(mine, mine, a2_send.at[f, i], a2_recv.at[f, i], device)

    def grad_second_wait(f, i):
        theirs = grad.at[other, lax.rem(x + 4 - i, 4), :, lanes(f)]
        remote(theirs, theirs, a2_send.at[f, i], a2_recv.at[f, i], tp_y).wait_recv()

    def draft(c):
        parts = CHUNKS[c][1]
        start, stop = parts[0][0], parts[-1][0] + parts[-1][1]
        while start < stop:
            step = min(256, stop - start)
            value = lax.dot_general(
                w_buf[...], hid[pl.ds(start, step), :], (((1,), (1,)), ((), ())),
                preferred_element_type=jnp.float32,
            )
            part[:, :, :, pl.ds(start, step)] = value.astype(jnp.bfloat16).reshape(
                part.shape[:3] + (step,)
            )
            start += step

    def peers(f, stage):
        return (1, 2, 3) if (PARTS[f][2] == "x") == (stage == 0) else (0,)

    def parts_of(c):
        return [f for f in range(len(PARTS)) if PARTS[f] in CHUNKS[c][1]]

    def start_first(c):
        draft(c)
        for f in parts_of(c):
            for i in peers(f, 0):
                sum_first(f, i).start()

    def start_second(c):
        for f in parts_of(c):
            n = lanes(f)
            for i in peers(f, 0):
                sum_first(f, i).wait_recv()
            if PARTS[f][2] == "x":

                def summed(g):
                    value = part[g, x, :, n].astype(jnp.float32)
                    for i in range(3):
                        value = value + first_x[i, g, :, n].astype(jnp.float32)
                    return value

                half[3, :, n] = summed(other).astype(jnp.bfloat16)
                sum_second(f, 0).start()
                own[:, n] = summed(y_lo)
            else:

                def summed(g):
                    return part[y_lo, g, :, n].astype(jnp.float32) + first_y[g, :, n].astype(
                        jnp.float32
                    )

                for i in range(1, 4):
                    half[i - 1, :, n] = summed(lax.rem(x + i, 4)).astype(jnp.bfloat16)
                    sum_second(f, i).start()
                own[:, n] = summed(x)

    def start_grad(c):
        for f in parts_of(c):
            n = lanes(f)
            value = own[:, n]
            for i in peers(f, 1):
                sum_second(f, i).wait_recv()
                value = value + second[(i - 1) % 4, :, n].astype(jnp.float32)
            value = (value - following[:, n]) / QLEN
            grad[y_lo, x, :, n] = value.astype(jnp.bfloat16)
            for i in range(4):
                grad_first(f, i).start()

    def forward_grad(c):
        for f in parts_of(c):
            if PARTS[f][2] == "x":
                grad_first_wait(f, 0)
                for i in range(1, 4):
                    grad_second(f, i).start()
            else:
                for i in range(1, 4):
                    grad_first_wait(f, i)
                    grad_second(f, i).start()

    def project(c, last):
        for f in parts_of(c):
            if PARTS[f][2] == "x":
                for i in range(1, 4):
                    grad_first_wait(f, i)
            else:
                grad_first_wait(f, 0)
            for i in range(1, 4):
                grad_second_wait(f, i)
        parts = CHUNKS[c][1]
        start = parts[0][0]
        rows = parts[-1][0] + parts[-1][1] - start
        tile = min(256, features)
        for n in range(features // tile):
            columns = pl.ds(n * tile, tile)
            value = jnp.dot(
                grad[:, :, :, pl.ds(start, rows)].reshape(total.shape[0], rows),
                hid[pl.ds(start, rows), columns],
                preferred_element_type=jnp.float32,
            )
            if c == 0:
                total[:, columns] = value
            else:
                total[:, columns] += value
            if last:
                out_copy(n).start()

    def out_copy(n):
        tile = min(256, features)
        span = (pl.ds(0, total.shape[0]), pl.ds(n * tile, tile))
        return pltpu.make_async_copy(total.at[span], out_ref.at[span], io_sem.at[3 + n])

    gather(2, 0).wait_recv()
    gather(3, 0).start()
    gather(1, 1).wait_recv()
    gather(3, 1).start()
    gather(2, 1).wait_recv()
    sibling(2).start()
    gather(1, 0).wait_recv()
    sibling(1).start()
    for p in range(2):
        gather(4, p).wait_recv()
        gather(6, p).start()
        gather(5, p).start()
    sibling(4).start()
    for p in range(2):
        gather(3, p).wait_recv()
    sibling(3).start()
    for k in CHUNKS[0][0]:
        sibling(k).wait_recv()
    start_first(0)
    gather(6, 0).wait_recv()
    gather(7, 0).start()
    gather(5, 1).wait_recv()
    gather(7, 1).start()
    gather(6, 1).wait_recv()
    sibling(6).start()
    gather(5, 0).wait_recv()
    sibling(5).start()
    for k, dc in foll_peers:
        foll_exchange(k, dc).start()
    for k in CHUNKS[1][0]:
        sibling(k).wait_recv()
    start_first(1)
    for p in range(2):
        gather(7, p).wait_recv()
    sibling(7).start()
    sibling(7).wait_recv()
    start_first(2)
    start_second(0)

    foll_copy.wait()
    for k, dc in foll_peers:
        foll_exchange(k, dc).wait_recv()
    for h in range(2):
        rows = jnp.concatenate([foll[8 * h + s] for s in range(8)], axis=1)
        following[:, pl.ds(h * half_rows, half_rows)] = jnp.dot(
            rows, place[...], preferred_element_type=jnp.float32
        )

    start_second(1)
    start_grad(0)
    start_second(2)
    forward_grad(0)
    start_grad(1)
    start_grad(2)
    forward_grad(1)
    forward_grad(2)
    project(0, False)
    project(1, False)
    project(2, True)

    for k in range(1, 8):
        for p in range(2):
            gather(k, p).wait_send()
    for k in range(8):
        sibling(k).wait_send()
    for k, dc in foll_peers:
        foll_exchange(k, dc).wait_send()
    for f in range(len(PARTS)):
        for i in peers(f, 0):
            sum_first(f, i).wait_send()
        for i in peers(f, 1):
            sum_second(f, i).wait_send()
        for i in range(4):
            grad_first(f, i).wait_send()
        for i in range(1, 4):
            grad_second(f, i).wait_send()
    for n in range(features // min(256, features)):
        out_copy(n).wait()


def gradient(used, foll, w_flat, n_tp):
    block, features = used.shape
    outs = w_flat.shape[0]
    width = outs // n_tp
    rows = 16 * block
    parts = len(PARTS)
    any_spec = pl.BlockSpec(memory_space=pl.ANY)
    dma = pltpu.SemaphoreType.DMA
    return pl.pallas_call(
        gradient_kernel,
        out_shape=jax.ShapeDtypeStruct((outs, features), jnp.float32),
        in_specs=[any_spec] * 3,
        out_specs=any_spec,
        scratch_shapes=[
            pltpu.VMEM((rows, features), jnp.bfloat16),
            pltpu.VMEM((outs, features), jnp.bfloat16),
            pltpu.VMEM((16, width, 128), jnp.bfloat16),
            pltpu.VMEM((8 * 128, rows // 2), jnp.bfloat16),
            pltpu.VMEM((width, rows), jnp.float32),
            pltpu.VMEM((2, 4, width, rows), jnp.bfloat16),
            pltpu.VMEM((3, 2, width, rows), jnp.bfloat16),
            pltpu.VMEM((4, width, rows), jnp.bfloat16),
            pltpu.VMEM((4, width, rows), jnp.bfloat16),
            pltpu.VMEM((width, rows), jnp.float32),
            pltpu.VMEM((4, width, rows), jnp.bfloat16),
            pltpu.VMEM((2, 4, width, rows), jnp.bfloat16),
            pltpu.VMEM((outs, features), jnp.float32),
            dma((7,)), dma((8, 2)), dma((8, 2)), dma((8,)), dma((8,)), dma((16,)), dma((16,)),
            dma((parts, 4)), dma((parts, 4)), dma((parts, 4)), dma((parts, 4)),
            dma((parts, 4)), dma((parts, 4)), dma((parts, 4)), dma((parts, 4)),
        ],
        compiler_params=pltpu.CompilerParams(
            collective_id=0, has_side_effects=True, vmem_limit_bytes=56 * 2**20
        ),
        name="gradient",
    )(used, foll, w_flat)


def shards(query, k_cache, v_cache, ctx_len, residual, accepted, w_draft):
    requests, new_tokens, heads, head_dim = query.shape
    slots = k_cache.shape[2]
    hidden, used, foll = attention(
        query.reshape(requests, new_tokens * heads, head_dim),
        k_cache.reshape(requests, slots, head_dim),
        v_cache.reshape(requests, slots, head_dim),
        ctx_len, residual, accepted,
    )
    features, groups, width = w_draft.shape
    w_flat = w_draft.transpose(1, 2, 0).reshape(groups * width, features)
    grad = gradient(used, foll, w_flat, groups)
    return hidden, grad.reshape(groups, width, features).transpose(2, 0, 1)


def solution(mesh):
    placed = (
        P("req", None, "tp", None),
        P("req", "tp", None, None),
        P("req", "tp", None, None),
        P("req"),
        P("req", "tp"),
        P(),
        P("tp", None, "req"),
    )
    return jax.shard_map(
        shards,
        mesh=mesh,
        in_specs=placed,
        out_specs=(P("req", "tp"), P("tp", None, "req")),
        check_vma=False,
    )
```

time: 85.9 us -> 62.3 us (0.73); the launches traced: 84.3 us -> 62.2 us
  Pallas kernels: 75.6 us -> 58.4 us
  local copies, waits for them, and re-layouts: 8.03 us -> 3.16 us
    pallas_call x1, Pallas kernels: 62.9 us -> 50.6 us  [gradient(): pl.pallas_call(gradient_kernel, out_shape=jax.ShapeDtypeStruct((outs, fea...]
    pallas_call x1, Pallas kernels: 12.7 us -> 7.77 us  [attention(): pl.pallas_call(attention_kernel, out_shape=(jax.ShapeDtypeStruct((all_row...]
    unnamed x13 -> x1, local copies, waits for them, and re-layouts: 8.03 us -> 3.16 us
where the time goes in v2:
time: 62.3 us; the launch traced here: 62.2 us
  Pallas kernels  58.4 us (94%)
  local copies, waits for them, and re-layouts  3.16 us (5%)
  between operations  0.65 us (1%)
    pallas_call x1, Pallas kernels, gradient(): pl.pallas_call(gradient_kernel, out_shape=jax.ShapeDtypeStruct((outs, fea...  50.6 us
    pallas_call x1, Pallas kernels, attention(): pl.pallas_call(attention_kernel, out_shape=(jax.ShapeDtypeStruct((all_row...  7.77 us
    unnamed x1, local copies, waits for them, and re-layouts  3.16 us

profile of v2, /device:TPU:0, one launch (start us, length us, event | category | flops | bytes accessed | tf_op | source)
XLA Modules:
  0.0 62.2 jit_solution(16573599120491319938)
XLA Ops:
  0.6 7.8 %attention.1 = (bf16[192,1024]{1,0:T(8,128)(2,1)}, bf16[80,1024]{1,0:T(8,128)(2,1)}, bf16[1024,128]{1,0:T(8,128)(2,1)}) custom-call(s32[32]{0:T(128)} %ctx_ref.1, s32[512]{0:T(512)} %accepted_ref.1, bf16[32,48,128]{2,1,0:T(8,128)(2,1)} %bitcast.13, bf16[32,1024,128]{2,1,0:T(8,128)(2,1)} %bitcast.10, bf16[32,1024,128]{2,1,0:T(8,128)(2,1)} %bitcast.11, ...), custom_call_target="tpu_custom_call" | custom-call | tf_op jit(solution)/shard_map/attention/pallas_call | solution.py:138
  8.4 50.6 %gradient.1 = f32[512,1024]{1,0:T(8,128)} custom-call(bf16[80,1024]{1,0:T(8,128)(2,1)} %get-tuple-element.6.used_ref, bf16[1024,128]{1,0:T(8,128)(2,1)} %get-tuple-element.7.foll_ref, bf16[512,1024]{1,0:T(8,128)(2,1)} %bitcast.12), custom_call_target="tpu_custom_call" | custom-call | tf_op jit(solution)/shard_map/gradient/pallas_call | solution.py:525
  59.0 3.2 %copy.10 = f32[1024,8,64]{0,2,1:T(8,128)} copy(f32[1024,8,64]{0,2,1:T(8,128)} %bitcast.9) | data formatting | bytes 4194304

commit v3 on v2

--- a/solution.py
+++ b/solution.py
@@ -34,12 +34,13 @@
 def attention_kernel(
     ctx_ref, accepted_ref, q_hbm, k_hbm, v_hbm, res_hbm,
     hidden_hbm, used_ref, foll_ref,
-    q_buf, k_buf, v_buf, res_buf, att_buf, hid_buf, k_sem, v_sem, k_more, v_more, io_sem,
+    q_buf, k_buf, v_buf, res_buf, att_buf, hid_buf, pick_buf, k_sem, v_sem, k_more, v_more, io_sem,
 ):
     requests, slots, head_dim = k_hbm.shape
     rows = q_buf.shape[1]
     scale = head_dim ** (-0.5)
     batches = requests // BATCH
+    all_rows = requests * QLEN
     q_copy = pltpu.make_async_copy(q_hbm, q_buf, io_sem.at[0])
     res_copy = pltpu.make_async_copy(res_hbm, res_buf, io_sem.at[1])
     q_copy.start()
@@ -69,37 +70,6 @@
         def _():
             for copy in more_copies(r):
                 copy.start()
-
-    q_copy.wait()
-
-    @pl.loop(0, batches)
-    def _(b):
-        for copy in short_copies(b):
-            copy.wait()
-        for j in range(BATCH):
-            r = b * BATCH + j
-            att_buf[pl.ds(pl.multiple_of(r * rows, rows), rows), :] = attend(
-                q_buf[r], k_buf[r, 0:SHORT], v_buf[r, 0:SHORT], ctx_ref[r], scale
-            )
-
-    @pl.loop(0, requests)
-    def _(r):
-        @pl.when(ctx_ref[r] > SHORT)
-        def _():
-            for copy in more_copies(r):
-                copy.wait()
-            att_buf[pl.ds(pl.multiple_of(r * rows, rows), rows), :] = attend(
-                q_buf[r], k_buf[r], v_buf[r], ctx_ref[r], scale
-            )
-
-    res_copy.wait()
-    all_rows = requests * QLEN
-    for h in range(GROUP):
-        columns = pl.ds(h * head_dim, head_dim)
-        mixed = att_buf[pl.ds(h, all_rows, stride=GROUP), :]
-        hid_buf[:, columns] = (res_buf[:, columns].astype(jnp.float32) + mixed).astype(jnp.bfloat16)
-    hidden_copy = pltpu.make_async_copy(hid_buf, hidden_hbm, io_sem.at[2])
-    hidden_copy.start()
 
     row = lax.broadcasted_iota(jnp.int32, (1, all_rows), 1)
     request = row // QLEN
@@ -116,14 +86,43 @@
             mine & (verified >= 1) & (verified <= count), before + verified - 1, next_place
         )
         before = before + count
+    want = lax.broadcasted_iota(jnp.int32, (used_ref.shape[0], all_rows), 0)
+    pick_buf[0] = (want == place).astype(jnp.float32).astype(jnp.bfloat16)
+    pick_buf[1] = (want == next_place).astype(jnp.float32).astype(jnp.bfloat16)
+
+    q_copy.wait()
+
+    @pl.loop(0, batches)
+    def _(b):
+        for copy in short_copies(b):
+            copy.wait()
+        for j in range(BATCH):
+            r = b * BATCH + j
+            att_buf[pl.ds(pl.multiple_of(r * rows, rows), rows), :] = attend(
+                q_buf[r], k_buf[r, 0:SHORT], v_buf[r, 0:SHORT], ctx_ref[r], scale
+            )
+
+    @pl.loop(0, requests)
+    def _(r):
+        @pl.when(ctx_ref[r] > SHORT)
+        def _():
+            for copy in more_copies(r):
+                copy.wait()
+            att_buf[pl.ds(pl.multiple_of(r * rows, rows), rows), :] = attend(
+                q_buf[r], k_buf[r], v_buf[r], ctx_ref[r], scale
+            )
+
+    res_copy.wait()
+    for h in range(GROUP):
+        columns = pl.ds(h * head_dim, head_dim)
+        mixed = att_buf[pl.ds(h, all_rows, stride=GROUP), :]
+        hid_buf[:, columns] = (res_buf[:, columns].astype(jnp.float32) + mixed).astype(jnp.bfloat16)
+    hidden_copy = pltpu.make_async_copy(hid_buf, hidden_hbm, io_sem.at[2])
+    hidden_copy.start()
+
     hidden = hid_buf[...]
-    want = lax.broadcasted_iota(jnp.int32, (used_ref.shape[0], all_rows), 0)
-    pick = (want == place).astype(jnp.float32).astype(jnp.bfloat16)
-    used_ref[...] = jnp.dot(pick, hidden, preferred_element_type=jnp.float32).astype(jnp.bfloat16)
-    want = lax.broadcasted_iota(jnp.int32, (foll_ref.shape[1], all_rows), 0)
-    pick = (want == next_place).astype(jnp.float32).astype(jnp.bfloat16)
-    following = jnp.dot(pick, hidden, preferred_element_type=jnp.float32)
-    foll_ref[...] = following.T.astype(jnp.bfloat16)
+    used_ref[...] = jnp.dot(pick_buf[0], hidden, preferred_element_type=jnp.float32).astype(jnp.bfloat16)
+    foll_ref[...] = jnp.dot(pick_buf[1], hidden, preferred_element_type=jnp.float32).astype(jnp.bfloat16)
     hidden_copy.wait()
 
 
@@ -131,7 +130,7 @@
     requests, slots, head_dim = k_cache.shape
     rows = query.shape[1]
     all_rows, features = residual.shape
-    any_spec = pl.BlockSpec(memory_space=pl.ANY)
+    hbm = pl.BlockSpec(memory_space=pl.ANY)
     smem = pl.BlockSpec(memory_space=pltpu.SMEM)
     vmem = pl.BlockSpec(memory_space=pltpu.VMEM)
     batches = requests // BATCH
@@ -140,10 +139,10 @@
         out_shape=(
             jax.ShapeDtypeStruct((all_rows, features), jnp.bfloat16),
             jax.ShapeDtypeStruct((USED_PER_BLOCK, features), jnp.bfloat16),
-            jax.ShapeDtypeStruct((features, 128), jnp.bfloat16),
+            jax.ShapeDtypeStruct((USED_PER_BLOCK, features), jnp.bfloat16),
         ),
-        in_specs=[smem, smem, any_spec, any_spec, any_spec, any_spec],
-        out_specs=(any_spec, vmem, vmem),
+        in_specs=[smem, smem, hbm, hbm, hbm, hbm],
+        out_specs=(hbm, vmem, vmem),
         scratch_shapes=[
             pltpu.VMEM((requests, rows, head_dim), jnp.bfloat16),
             pltpu.VMEM((requests, slots, head_dim), jnp.bfloat16),
@@ -151,32 +150,36 @@
             pltpu.VMEM((all_rows, features), jnp.bfloat16),
             pltpu.VMEM((requests * rows, head_dim), jnp.float32),
             pltpu.VMEM((all_rows, features), jnp.bfloat16),
+            pltpu.VMEM((2, USED_PER_BLOCK, all_rows), jnp.bfloat16),
             pltpu.SemaphoreType.DMA((batches,)),
             pltpu.SemaphoreType.DMA((batches,)),
             pltpu.SemaphoreType.DMA((requests,)),
             pltpu.SemaphoreType.DMA((requests,)),
             pltpu.SemaphoreType.DMA((3,)),
         ],
-        compiler_params=pltpu.CompilerParams(vmem_limit_bytes=60 * 2**20),
+        compiler_params=pltpu.CompilerParams(vmem_limit_bytes=58 * 2**20),
         name="attention",
     )(ctx_len, accepted, query, k_cache, v_cache, residual)
 
 
-SOURCES = ((0, 0), (0, 1), (0, 3), (0, 2), (1, 0), (1, 1), (1, 3), (1, 2))
-PIECES = ((0, 48), (48, 32))
+SOURCES = ((0, 0), (0, 1), (0, 3), (1, 0), (0, 2), (1, 1), (1, 3), (1, 2))
 CHUNKS = (
-    ((0, 1, 2, 3), ((0, 384, "x"), (384, 256, "y"))),
+    ((0,), ((0, 128, "x"),)),
+    ((1, 2, 3), ((128, 256, "x"), (384, 256, "y"))),
     ((4, 5, 6), ((640, 256, "x"), (896, 128, "y"))),
     ((7,), ((1024, 128, "x"), (1152, 128, "y"))),
 )
+PIECES = ((0, 48), (48, 32))
 PARTS = tuple(part for _, parts in CHUNKS for part in parts)
+DIRECT = (2, 6, 4, 5, 7, 1, 3)
 
 
 def gradient_kernel(
     used_ref, foll_ref, w_ref, out_ref,
-    hid, w_buf, foll, place, following, part, first_x, first_y, half, own, second, grad, total,
+    hid, w_buf, foll, following, part, first_x, first_y, half, own, second, direct, grad, total,
     io_sem, g_send, g_recv, sib_send, sib_recv, fo_send, fo_recv,
     s1_send, s1_recv, s2_send, s2_recv, a1_send, a1_recv, a2_send, a2_recv,
+    d1_send, d1_recv, d2_send, d2_recv,
 ):
     r = lax.axis_index("req")
     t = lax.axis_index("tp")
@@ -187,7 +190,7 @@
     y_lo = t // 4
     other = 1 - y_lo
     block, features = used_ref.shape
-    width = foll.shape[1]
+    width = part.shape[2]
     rows_all = hid.shape[0]
 
     def req_at(dy, dz, dc):
@@ -197,6 +200,9 @@
         return {"tp": y_lo * 4 + lax.rem(x + i, 4)}
 
     tp_y = {"tp": other * 4 + x}
+
+    def tp_diagonal(i):
+        return {"tp": other * 4 + lax.rem(x + i, 4)}
 
     def remote(src, dst, send, recv, device):
         return pltpu.make_async_remote_copy(
@@ -207,7 +213,9 @@
     w_copy = pltpu.make_async_copy(w_ref, w_buf, io_sem.at[0])
     own_copy = pltpu.make_async_copy(used_ref, hid.at[pl.ds(0, block)], io_sem.at[1])
     foll_copy = pltpu.make_async_copy(
-        foll_ref.at[pl.ds(pl.multiple_of(r * width, width), width)], foll.at[0], io_sem.at[2]
+        foll_ref.at[:, pl.ds(pl.multiple_of(r // 2 * 128, 128), 128)],
+        foll.at[pl.ds(0, block)],
+        io_sem.at[2],
     )
     own_copy.start()
     w_copy.start()
@@ -215,39 +223,33 @@
 
     barrier = pltpu.get_barrier_semaphore()
     for dy, dz in SOURCES:
-        for dc in range(2):
-            if (dy, dz, dc) != (0, 0, 0):
-                pl.semaphore_signal(
-                    barrier, inc=1, device_id={"req": req_at(dy, dz, dc)}, device_id_type=MESH
-                )
+        dc = int((dy, dz) == (0, 0))
+        pl.semaphore_signal(
+            barrier, inc=1, device_id={"req": req_at(dy, dz, dc)}, device_id_type=MESH
+        )
     for i in range(1, 4):
         pl.semaphore_signal(barrier, inc=1, device_id=tp_x(i), device_id_type=MESH)
+        pl.semaphore_signal(barrier, inc=1, device_id=tp_diagonal(i), device_id_type=MESH)
     pl.semaphore_signal(barrier, inc=1, device_id=tp_y, device_id_type=MESH)
-    pl.semaphore_wait(barrier, 19)
+    pl.semaphore_wait(barrier, 15)
+
+    up, down, across = (0, 1), (0, -1), (1, 0)
+    routes = {
+        1: ((0, down), (0, down)), 2: ((0, up), (0, up)), 3: ((0, across), (0, across)),
+        4: ((2, up), (1, down)), 5: ((3, down), (3, down)), 6: ((3, up), (3, up)),
+        7: ((6, up), (5, down)),
+    }
 
     def shard(k, p):
         start, rows = PIECES[p]
         return hid.at[pl.ds(2 * block * k + start, rows)]
 
     def gather(k, p):
+        source, target = routes[k][p]
         start, rows = PIECES[p]
-        mine = used_ref.at[pl.ds(start, rows)]
-        if k == 1:
-            src, target = mine, (0, -1)
-        elif k == 2:
-            src, target = mine, (0, 1)
-        elif k == 3:
-            src, target = (shard(2, 0), (0, 1)) if p == 0 else (shard(1, 1), (0, -1))
-        elif k == 4:
-            src, target = mine, (1, 0)
-        elif k == 5:
-            src, target = shard(4, p), (0, -1)
-        elif k == 6:
-            src, target = shard(4, p), (0, 1)
-        else:
-            src, target = (shard(6, 0), (0, 1)) if p == 0 else (shard(5, 1), (0, -1))
         return remote(
-            src, shard(k, p), g_send.at[k, p], g_recv.at[k, p], {"req": req_at(*target, 0)}
+            shard(source, p) if source else used_ref.at[pl.ds(start, rows)], shard(k, p),
+            g_send.at[k, p], g_recv.at[k, p], {"req": req_at(*target, 0)},
         )
 
     def sibling(k):
@@ -258,31 +260,29 @@
     for p in range(2):
         gather(2, p).start()
         gather(1, 1 - p).start()
-        gather(4, p).start()
+        gather(3, p).start()
     sibling(0).start()
-
-    half_rows = rows_all // 2
-
-    @pl.loop(0, 8)
-    def _(s):
-        j = lax.broadcasted_iota(jnp.int32, (128, half_rows), 0)
-        column = lax.broadcasted_iota(jnp.int32, (128, half_rows), 1)
-        hit = (column == s * block + j) & (j < block)
-        place[pl.ds(pl.multiple_of(s * 128, 128), 128), :] = hit.astype(jnp.float32).astype(
-            jnp.bfloat16
-        )
 
     own_copy.wait()
     w_copy.wait()
 
-    def foll_exchange(k, dc):
+    def foll_rows(j):
+        return foll.at[pl.ds(j * block, block)]
+
+    def foll_exchange(k):
         dy, dz = SOURCES[k]
-        target = req_at(dy, -dz, dc)
-        src = foll_ref.at[pl.ds(pl.multiple_of(target * width, width), width)]
-        j = 2 * k + dc
-        return remote(src, foll.at[j], fo_send.at[j], fo_recv.at[j], {"req": target})
-
-    foll_peers = [(k, dc) for k in range(8) for dc in range(2) if (k, dc) != (0, 0)]
+        chip = lax.rem(y_hi + dy, 2) * 4 + lax.rem(z + 4 - dz, 4)
+        src = foll_ref.at[:, pl.ds(pl.multiple_of(chip * 128, 128), 128)]
+        return remote(
+            src, foll_rows(2 * k), fo_send.at[2 * k], fo_recv.at[2 * k],
+            {"req": req_at(dy, -dz, 0)},
+        )
+
+    def foll_sibling(k):
+        j = 2 * k + 1
+        return remote(
+            foll_rows(2 * k), foll_rows(j), fo_send.at[j], fo_recv.at[j], {"req": req_at(0, 0, 1)}
+        )
 
     def lanes(f):
         return pl.ds(PARTS[f][0], PARTS[f][1])
@@ -295,6 +295,25 @@
             )
         src = part.at[other, :, :, lanes(f)]
         return remote(src, first_y.at[:, :, lanes(f)], s1_send.at[f, 0], s1_recv.at[f, 0], tp_y)
+
+    def sum_direct(f, i):
+        row, column = (y_lo, other)[i // 4], lax.rem(x + i, 4)
+        src, dst = part.at[row, column, :, lanes(f)], direct.at[i - 1, :, lanes(f)]
+        return remote(src, dst, d1_send.at[f, i], d1_recv.at[f, i], tp_at(i))
+
+    def grad_direct(f, i):
+        mine = grad.at[y_lo, x, :, lanes(f)]
+        return remote(mine, mine, d2_send.at[f, i], d2_recv.at[f, i], tp_at(i))
+
+    def grad_direct_wait(f, i):
+        theirs = grad.at[(y_lo, other)[i // 4], lax.rem(x + 8 - i, 4), :, lanes(f)]
+        remote(theirs, theirs, d2_send.at[f, i], d2_recv.at[f, i], tp_at(i)).wait_recv()
+
+    def tp_at(i):
+        return {"tp": (y_lo, other)[i // 4] * 4 + lax.rem(x + i, 4)}
+
+    def is_direct(f):
+        return PARTS[f][2] == "d"
 
     def sum_second(f, i):
         slot = (i - 1) % 4
@@ -340,6 +359,8 @@
             start += step
 
     def peers(f, stage):
+        if is_direct(f):
+            return ()
         return (1, 2, 3) if (PARTS[f][2] == "x") == (stage == 0) else (0,)
 
     def parts_of(c):
@@ -350,10 +371,15 @@
         for f in parts_of(c):
             for i in peers(f, 0):
                 sum_first(f, i).start()
+            if is_direct(f):
+                for i in DIRECT:
+                    sum_direct(f, i).start()
 
     def start_second(c):
         for f in parts_of(c):
             n = lanes(f)
+            if is_direct(f):
+                continue
             for i in peers(f, 0):
                 sum_first(f, i).wait_recv()
             if PARTS[f][2] == "x":
@@ -382,17 +408,29 @@
     def start_grad(c):
         for f in parts_of(c):
             n = lanes(f)
-            value = own[:, n]
+            if is_direct(f):
+                value = part[y_lo, x, :, n].astype(jnp.float32)
+                for i in DIRECT:
+                    sum_direct(f, i).wait_recv()
+                    value = value + direct[i - 1, :, n].astype(jnp.float32)
+            else:
+                value = own[:, n]
             for i in peers(f, 1):
                 sum_second(f, i).wait_recv()
                 value = value + second[(i - 1) % 4, :, n].astype(jnp.float32)
             value = (value - following[:, n]) / QLEN
             grad[y_lo, x, :, n] = value.astype(jnp.bfloat16)
+            if is_direct(f):
+                for i in DIRECT:
+                    grad_direct(f, i).start()
+                continue
             for i in range(4):
                 grad_first(f, i).start()
 
     def forward_grad(c):
         for f in parts_of(c):
+            if is_direct(f):
+                continue
             if PARTS[f][2] == "x":
                 grad_first_wait(f, 0)
                 for i in range(1, 4):
@@ -402,8 +440,12 @@
                     grad_first_wait(f, i)
                     grad_second(f, i).start()
 
-    def project(c, last):
+    def project(c):
         for f in parts_of(c):
+            if is_direct(f):
+                for i in DIRECT:
+                    grad_direct_wait(f, i)
+                continue
             if PARTS[f][2] == "x":
                 for i in range(1, 4):
                     grad_first_wait(f, i)
@@ -411,9 +453,7 @@
                 grad_first_wait(f, 0)
             for i in range(1, 4):
                 grad_second_wait(f, i)
-        parts = CHUNKS[c][1]
-        start = parts[0][0]
-        rows = parts[-1][0] + parts[-1][1] - start
+        start, rows = span_of(c)
         tile = min(256, features)
         for n in range(features // tile):
             columns = pl.ds(n * tile, tile)
@@ -426,33 +466,50 @@
                 total[:, columns] = value
             else:
                 total[:, columns] += value
-            if last:
+            if c == len(CHUNKS) - 1:
                 out_copy(n).start()
+
+    def span_of(c):
+        parts = CHUNKS[c][1]
+        return parts[0][0], parts[-1][0] + parts[-1][1] - parts[0][0]
 
     def out_copy(n):
         tile = min(256, features)
         span = (pl.ds(0, total.shape[0]), pl.ds(n * tile, tile))
         return pltpu.make_async_copy(total.at[span], out_ref.at[span], io_sem.at[3 + n])
 
+    def arrive(c):
+        for k in CHUNKS[c][0]:
+            sibling(k).wait_recv()
+
+    def following_of(half):
+        span = rows_all // 2
+        rows = foll[pl.ds(half * span, span), :].astype(jnp.float32).T
+        return jnp.where(core == 0, rows[:width], rows[width:])
+
+    arrive(0)
+    start_first(0)
     gather(2, 0).wait_recv()
-    gather(3, 0).start()
+    gather(4, 0).start()
     gather(1, 1).wait_recv()
-    gather(3, 1).start()
+    gather(4, 1).start()
     gather(2, 1).wait_recv()
     sibling(2).start()
     gather(1, 0).wait_recv()
     sibling(1).start()
     for p in range(2):
-        gather(4, p).wait_recv()
+        gather(3, p).wait_recv()
         gather(6, p).start()
         gather(5, p).start()
+    sibling(3).start()
+    start_second(0)
+    arrive(1)
+    start_first(1)
+    for k in range(1, 8):
+        foll_exchange(k).start()
+    for p in range(2):
+        gather(4, p).wait_recv()
     sibling(4).start()
-    for p in range(2):
-        gather(3, p).wait_recv()
-    sibling(3).start()
-    for k in CHUNKS[0][0]:
-        sibling(k).wait_recv()
-    start_first(0)
     gather(6, 0).wait_recv()
     gather(7, 0).start()
     gather(5, 1).wait_recv()
@@ -461,47 +518,51 @@
     sibling(6).start()
     gather(5, 0).wait_recv()
     sibling(5).start()
-    for k, dc in foll_peers:
-        foll_exchange(k, dc).start()
-    for k in CHUNKS[1][0]:
-        sibling(k).wait_recv()
-    start_first(1)
+    arrive(2)
+    start_first(2)
+    start_second(1)
+    foll_copy.wait()
+    foll_sibling(0).start()
+    for k in range(1, 8):
+        foll_exchange(k).wait_recv()
+        foll_sibling(k).start()
     for p in range(2):
         gather(7, p).wait_recv()
     sibling(7).start()
-    sibling(7).wait_recv()
-    start_first(2)
-    start_second(0)
-
-    foll_copy.wait()
-    for k, dc in foll_peers:
-        foll_exchange(k, dc).wait_recv()
+    for k in range(8):
+        foll_sibling(k).wait_recv()
     for h in range(2):
-        rows = jnp.concatenate([foll[8 * h + s] for s in range(8)], axis=1)
-        following[:, pl.ds(h * half_rows, half_rows)] = jnp.dot(
-            rows, place[...], preferred_element_type=jnp.float32
-        )
-
-    start_second(1)
+        following[:, pl.ds(h * (rows_all // 2), rows_all // 2)] = following_of(h)
     start_grad(0)
+    arrive(3)
+    start_first(3)
+    start_grad(1)
     start_second(2)
     forward_grad(0)
-    start_grad(1)
+    start_second(3)
+    forward_grad(1)
     start_grad(2)
-    forward_grad(1)
+    start_grad(3)
     forward_grad(2)
-    project(0, False)
-    project(1, False)
-    project(2, True)
+    forward_grad(3)
+    for c in range(len(CHUNKS)):
+        project(c)
 
     for k in range(1, 8):
         for p in range(2):
             gather(k, p).wait_send()
     for k in range(8):
         sibling(k).wait_send()
-    for k, dc in foll_peers:
-        foll_exchange(k, dc).wait_send()
+    for k in range(8):
+        if k:
+            foll_exchange(k).wait_send()
+        foll_sibling(k).wait_send()
     for f in range(len(PARTS)):
+        if is_direct(f):
+            for i in DIRECT:
+                sum_direct(f, i).wait_send()
+                grad_direct(f, i).wait_send()
+            continue
         for i in peers(f, 0):
             sum_first(f, i).wait_send()
         for i in peers(f, 1):
@@ -530,8 +591,7 @@
         scratch_shapes=[
             pltpu.VMEM((rows, features), jnp.bfloat16),
             pltpu.VMEM((outs, features), jnp.bfloat16),
-            pltpu.VMEM((16, width, 128), jnp.bfloat16),
-            pltpu.VMEM((8 * 128, rows // 2), jnp.bfloat16),
+            pltpu.VMEM((rows, 128), jnp.bfloat16),
             pltpu.VMEM((width, rows), jnp.float32),
             pltpu.VMEM((2, 4, width, rows), jnp.bfloat16),
             pltpu.VMEM((3, 2, width, rows), jnp.bfloat16),
@@ -539,14 +599,16 @@
             pltpu.VMEM((4, width, rows), jnp.bfloat16),
             pltpu.VMEM((width, rows), jnp.float32),
             pltpu.VMEM((4, width, rows), jnp.bfloat16),
+            pltpu.VMEM((7, width, rows), jnp.bfloat16),
             pltpu.VMEM((2, 4, width, rows), jnp.bfloat16),
             pltpu.VMEM((outs, features), jnp.float32),
             dma((7,)), dma((8, 2)), dma((8, 2)), dma((8,)), dma((8,)), dma((16,)), dma((16,)),
             dma((parts, 4)), dma((parts, 4)), dma((parts, 4)), dma((parts, 4)),
             dma((parts, 4)), dma((parts, 4)), dma((parts, 4)), dma((parts, 4)),
+            dma((parts, 8)), dma((parts, 8)), dma((parts, 8)), dma((parts, 8)),
         ],
         compiler_params=pltpu.CompilerParams(
-            collective_id=0, has_side_effects=True, vmem_limit_bytes=56 * 2**20
+            collective_id=0, has_side_effects=True, vmem_limit_bytes=58 * 2**20
         ),
         name="gradient",
     )(used, foll, w_flat)

time: 62.3 us -> 60.9 us (0.978)
  Pallas kernels: 58.4 us -> 57 us
    pallas_call x1, Pallas kernels: 50.6 us -> 49.9 us  [gradient(): pl.pallas_call(gradient_kernel, out_shape=jax.ShapeDtypeStruct((outs, fea...]
    pallas_call x1, Pallas kernels: 7.77 us -> 7.1 us  [attention(): pl.pallas_call(attention_kernel, out_shape=(jax.ShapeDtypeStruct((all_row...]
where the time goes in v3:
time: 60.9 us; the launch traced here: 60.8 us
  Pallas kernels  57 us (94%)
  local copies, waits for them, and re-layouts  3.16 us (5%)
  between operations  0.65 us (1%)
    pallas_call x1, Pallas kernels, gradient(): pl.pallas_call(gradient_kernel, out_shape=jax.ShapeDtypeStruct((outs, fea...  49.9 us
    pallas_call x1, Pallas kernels, attention(): pl.pallas_call(attention_kernel, out_shape=(jax.ShapeDtypeStruct((all_row...  7.1 us
    unnamed x1, local copies, waits for them, and re-layouts  3.16 us

profile of v3, /device:TPU:0, one launch (start us, length us, event | category | flops | bytes accessed | tf_op | source)
XLA Modules:
  0.0 60.8 jit_solution(8406163293114834919)
XLA Ops:
  0.6 7.1 %attention.1 = (bf16[192,1024]{1,0:T(8,128)(2,1)}, bf16[80,1024]{1,0:T(8,128)(2,1)}, bf16[80,1024]{1,0:T(8,128)(2,1)}) custom-call(s32[32]{0:T(128)} %ctx_ref.1, s32[512]{0:T(512)} %accepted_ref.1, bf16[32,48,128]{2,1,0:T(8,128)(2,1)} %bitcast.13, bf16[32,1024,128]{2,1,0:T(8,128)(2,1)} %bitcast.9, bf16[32,1024,128]{2,1,0:T(8,128)(2,1)} %bitcast.10, ...), custom_call_target="tpu_custom_call" | custom-call | tf_op jit(solution)/shard_map/attention/pallas_call | solution.py:137
  7.7 49.9 %gradient.1 = f32[512,1024]{1,0:T(8,128)} custom-call(bf16[80,1024]{1,0:T(8,128)(2,1)} %get-tuple-element.6.used_ref, bf16[80,1024]{1,0:T(8,128)(2,1)} %get-tuple-element.7.foll_ref, bf16[512,1024]{1,0:T(8,128)(2,1)} %bitcast.12), custom_call_target="tpu_custom_call" | custom-call | tf_op jit(solution)/shard_map/gradient/pallas_call | solution.py:586
  57.6 3.2 %copy.10 = f32[1024,8,64]{0,2,1:T(8,128)} copy(f32[1024,8,64]{0,2,1:T(8,128)} %bitcast.11) | data formatting | bytes 4194304

commit v4 on v3

--- a/solution.py
+++ b/solution.py
@@ -614,6 +614,40 @@
     )(used, foll, w_flat)
 
 
+WRITES = 8
+
+
+def write_kernel(in_ref, out_ref, buf, sem):
+    rows = in_ref.shape[0] // WRITES
+
+    def piece(n, out):
+        span = pl.ds(n * rows, rows)
+        if out:
+            return pltpu.make_async_copy(buf.at[span], out_ref.at[span], sem.at[1, n])
+        return pltpu.make_async_copy(in_ref.at[span], buf.at[span], sem.at[0, n])
+
+    for n in range(WRITES):
+        piece(n, False).start()
+    for n in range(WRITES):
+        piece(n, False).wait()
+        piece(n, True).start()
+    for n in range(WRITES):
+        piece(n, True).wait()
+
+
+def write(grad):
+    any_spec = pl.BlockSpec(memory_space=pl.ANY)
+    return pl.pallas_call(
+        write_kernel,
+        out_shape=jax.ShapeDtypeStruct(grad.shape, grad.dtype),
+        in_specs=[any_spec],
+        out_specs=any_spec,
+        scratch_shapes=[pltpu.VMEM(grad.shape, grad.dtype), pltpu.SemaphoreType.DMA((2, WRITES))],
+        compiler_params=pltpu.CompilerParams(vmem_limit_bytes=58 * 2**20),
+        name="write",
+    )(grad)
+
+
 def shards(query, k_cache, v_cache, ctx_len, residual, accepted, w_draft):
     requests, new_tokens, heads, head_dim = query.shape
     slots = k_cache.shape[2]
@@ -625,7 +659,7 @@
     )
     features, groups, width = w_draft.shape
     w_flat = w_draft.transpose(1, 2, 0).reshape(groups * width, features)
-    grad = gradient(used, foll, w_flat, groups)
+    grad = write(gradient(used, foll, w_flat, groups))
     return hidden, grad.reshape(groups, width, features).transpose(2, 0, 1)
 
 

time: 60.9 us -> 59.6 us (0.979)
  local copies, waits for them, and re-layouts: 3.16 us -> 0 us
  Pallas kernels: 57 us -> 58.8 us
    unnamed x1 -> x0, local copies, waits for them, and re-layouts: 3.16 us -> none
    pallas_call x0 -> x1, Pallas kernels: none -> 2.4 us  [write(): pl.pallas_call(write_kernel, out_shape=jax.ShapeDtypeStruct(grad.shape, g...]
    pallas_call x1, Pallas kernels: 49.9 us -> 48.7 us  [gradient(): pl.pallas_call(gradient_kernel, out_shape=jax.ShapeDtypeStruct((outs, fea...]
where the time goes in v4:
time: 59.6 us; the launch traced here: 59.4 us
  Pallas kernels  58.8 us (99%)
  between operations  0.65 us (1%)
    pallas_call x1, Pallas kernels, gradient(): pl.pallas_call(gradient_kernel, out_shape=jax.ShapeDtypeStruct((outs, fea...  48.7 us
    pallas_call x1, Pallas kernels, attention(): pl.pallas_call(attention_kernel, out_shape=(jax.ShapeDtypeStruct((all_row...  7.67 us
    pallas_call x1, Pallas kernels, write(): pl.pallas_call(write_kernel, out_shape=jax.ShapeDtypeStruct(grad.shape, g...  2.4 us

profile of v4, /device:TPU:0, one launch (start us, length us, event | category | flops | bytes accessed | tf_op | source)
XLA Modules:
  0.0 59.4 jit_solution(14185868952989218991)
XLA Ops:
  0.6 7.7 %attention.1 = (bf16[192,1024]{1,0:T(8,128)(2,1)}, bf16[80,1024]{1,0:T(8,128)(2,1)}, bf16[80,1024]{1,0:T(8,128)(2,1)}) custom-call(s32[32]{0:T(128)} %ctx_ref.1, s32[512]{0:T(512)} %accepted_ref.1, bf16[32,48,128]{2,1,0:T(8,128)(2,1)} %bitcast.13, bf16[32,1024,128]{2,1,0:T(8,128)(2,1)} %bitcast.9, bf16[32,1024,128]{2,1,0:T(8,128)(2,1)} %bitcast.10, ...), custom_call_target="tpu_custom_call" | custom-call | tf_op jit(solution)/shard_map/attention/pallas_call | solution.py:137
  8.3 48.7 %gradient.1.in_ref = f32[512,1024]{1,0:T(8,128)} custom-call(bf16[80,1024]{1,0:T(8,128)(2,1)} %get-tuple-element.6.used_ref, bf16[80,1024]{1,0:T(8,128)(2,1)} %get-tuple-element.7.foll_ref, bf16[512,1024]{1,0:T(8,128)(2,1)} %bitcast.12), custom_call_target="tpu_custom_call" | custom-call | tf_op jit(solution)/shard_map/gradient/pallas_call | solution.py:586
  57.0 2.4 %write.1 = f32[512,1024]{1,0:T(8,128)} custom-call(f32[512,1024]{1,0:T(8,128)} %gradient.1.in_ref), custom_call_target="tpu_custom_call" | custom-call | tf_op jit(solution)/shard_map/write/pallas_call | solution.py:640

commit v5 on v4

--- a/solution.py
+++ b/solution.py
@@ -148,7 +148,7 @@
             pltpu.VMEM((requests, slots, head_dim), jnp.bfloat16),
             pltpu.VMEM((requests, slots, head_dim), jnp.bfloat16),
             pltpu.VMEM((all_rows, features), jnp.bfloat16),
-            pltpu.VMEM((requests * rows, head_dim), jnp.float32),
+            pltpu.VMEM((requests * rows + GROUP, head_dim), jnp.float32),
             pltpu.VMEM((all_rows, features), jnp.bfloat16),
             pltpu.VMEM((2, USED_PER_BLOCK, all_rows), jnp.bfloat16),
             pltpu.SemaphoreType.DMA((batches,)),

time: 59.6 us -> 61.8 us (1.037)
  Pallas kernels: 58.8 us -> 60.4 us
    pallas_call x1, Pallas kernels: 48.7 us -> 50.9 us  [gradient(): pl.pallas_call(gradient_kernel, out_shape=jax.ShapeDtypeStruct((outs, fea...]
where the time goes in v5:
time: 61.8 us; the launch traced here: 61 us
  Pallas kernels  60.4 us (98%)
  between operations  0.65 us (1%)
    pallas_call x1, Pallas kernels, gradient(): pl.pallas_call(gradient_kernel, out_shape=jax.ShapeDtypeStruct((outs, fea...  50.9 us
    pallas_call x1, Pallas kernels, attention(): pl.pallas_call(attention_kernel, out_shape=(jax.ShapeDtypeStruct((all_row...  7.1 us
    pallas_call x1, Pallas kernels, write(): pl.pallas_call(write_kernel, out_shape=jax.ShapeDtypeStruct(grad.shape, g...  2.4 us

profile of v5, /device:TPU:0, one launch (start us, length us, event | category | flops | bytes accessed | tf_op | source)
XLA Modules:
  0.0 61.0 jit_solution(8364833533475091359)
XLA Ops:
  0.6 7.1 %attention.1 = (bf16[192,1024]{1,0:T(8,128)(2,1)}, bf16[80,1024]{1,0:T(8,128)(2,1)}, bf16[80,1024]{1,0:T(8,128)(2,1)}) custom-call(s32[32]{0:T(128)} %ctx_ref.1, s32[512]{0:T(512)} %accepted_ref.1, bf16[32,48,128]{2,1,0:T(8,128)(2,1)} %bitcast.13, bf16[32,1024,128]{2,1,0:T(8,128)(2,1)} %bitcast.9, bf16[32,1024,128]{2,1,0:T(8,128)(2,1)} %bitcast.10, ...), custom_call_target="tpu_custom_call" | custom-call | tf_op jit(solution)/shard_map/attention/pallas_call | solution.py:137
  7.7 50.9 %gradient.1.in_ref = f32[512,1024]{1,0:T(8,128)} custom-call(bf16[80,1024]{1,0:T(8,128)(2,1)} %get-tuple-element.6.used_ref, bf16[80,1024]{1,0:T(8,128)(2,1)} %get-tuple-element.7.foll_ref, bf16[512,1024]{1,0:T(8,128)(2,1)} %bitcast.12), custom_call_target="tpu_custom_call" | custom-call | tf_op jit(solution)/shard_map/gradient/pallas_call | solution.py:586
  58.6 2.4 %write.1 = f32[512,1024]{1,0:T(8,128)} custom-call(f32[512,1024]{1,0:T(8,128)} %gradient.1.in_ref), custom_call_target="tpu_custom_call" | custom-call | tf_op jit(solution)/shard_map/write/pallas_call | solution.py:640

commit v6 on v5

--- a/solution.py
+++ b/solution.py
@@ -33,8 +33,8 @@
 
 def attention_kernel(
     ctx_ref, accepted_ref, q_hbm, k_hbm, v_hbm, res_hbm,
-    hidden_hbm, used_ref, foll_ref,
-    q_buf, k_buf, v_buf, res_buf, att_buf, hid_buf, pick_buf, k_sem, v_sem, k_more, v_more, io_sem,
+    hidden_hbm, used_hbm, foll_hbm,
+    q_buf, k_buf, v_buf, res_buf, att_buf, hid_buf, pick_buf, rows_buf, k_sem, v_sem, k_more, v_more, io_sem,
 ):
     requests, slots, head_dim = k_hbm.shape
     rows = q_buf.shape[1]
@@ -86,7 +86,7 @@
             mine & (verified >= 1) & (verified <= count), before + verified - 1, next_place
         )
         before = before + count
-    want = lax.broadcasted_iota(jnp.int32, (used_ref.shape[0], all_rows), 0)
+    want = lax.broadcasted_iota(jnp.int32, (USED_PER_BLOCK, all_rows), 0)
     pick_buf[0] = (want == place).astype(jnp.float32).astype(jnp.bfloat16)
     pick_buf[1] = (want == next_place).astype(jnp.float32).astype(jnp.bfloat16)
 
@@ -121,9 +121,15 @@
     hidden_copy.start()
 
     hidden = hid_buf[...]
-    used_ref[...] = jnp.dot(pick_buf[0], hidden, preferred_element_type=jnp.float32).astype(jnp.bfloat16)
-    foll_ref[...] = jnp.dot(pick_buf[1], hidden, preferred_element_type=jnp.float32).astype(jnp.bfloat16)
-    hidden_copy.wait()
+    copies = [hidden_copy]
+    for i, out in enumerate((used_hbm, foll_hbm)):
+        rows_buf[i] = jnp.dot(
+            pick_buf[i], hidden, preferred_element_type=jnp.float32
+        ).astype(jnp.bfloat16)
+        copies.append(pltpu.make_async_copy(rows_buf.at[i], out, io_sem.at[3 + i]))
+        copies[-1].start()
+    for copy in copies:
+        copy.wait()
 
 
 def attention(query, k_cache, v_cache, ctx_len, residual, accepted):
@@ -132,7 +138,6 @@
     all_rows, features = residual.shape
     hbm = pl.BlockSpec(memory_space=pl.ANY)
     smem = pl.BlockSpec(memory_space=pltpu.SMEM)
-    vmem = pl.BlockSpec(memory_space=pltpu.VMEM)
     batches = requests // BATCH
     return pl.pallas_call(
         attention_kernel,
@@ -142,7 +147,7 @@
             jax.ShapeDtypeStruct((USED_PER_BLOCK, features), jnp.bfloat16),
         ),
         in_specs=[smem, smem, hbm, hbm, hbm, hbm],
-        out_specs=(hbm, vmem, vmem),
+        out_specs=(hbm, hbm, hbm),
         scratch_shapes=[
             pltpu.VMEM((requests, rows, head_dim), jnp.bfloat16),
             pltpu.VMEM((requests, slots, head_dim), jnp.bfloat16),
@@ -151,11 +156,12 @@
             pltpu.VMEM((requests * rows + GROUP, head_dim), jnp.float32),
             pltpu.VMEM((all_rows, features), jnp.bfloat16),
             pltpu.VMEM((2, USED_PER_BLOCK, all_rows), jnp.bfloat16),
+            pltpu.VMEM((2, USED_PER_BLOCK, features), jnp.bfloat16),
             pltpu.SemaphoreType.DMA((batches,)),
             pltpu.SemaphoreType.DMA((batches,)),
             pltpu.SemaphoreType.DMA((requests,)),
             pltpu.SemaphoreType.DMA((requests,)),
-            pltpu.SemaphoreType.DMA((3,)),
+            pltpu.SemaphoreType.DMA((5,)),
         ],
         compiler_params=pltpu.CompilerParams(vmem_limit_bytes=58 * 2**20),
         name="attention",

time: 61.8 us -> 60.1 us (0.972)
  Pallas kernels: 60.4 us -> 58.3 us
    pallas_call x1, Pallas kernels: 50.9 us -> 49.3 us  [gradient(): pl.pallas_call(gradient_kernel, out_shape=jax.ShapeDtypeStruct((outs, fea...]
where the time goes in v6:
time: 60.1 us; the launch traced here: 58.9 us
  Pallas kernels  58.3 us (97%)
  between operations  0.65 us (1%)
    pallas_call x1, Pallas kernels, gradient(): pl.pallas_call(gradient_kernel, out_shape=jax.ShapeDtypeStruct((outs, fea...  49.3 us
    pallas_call x1, Pallas kernels, attention(): pl.pallas_call(attention_kernel, out_shape=(jax.ShapeDtypeStruct((all_row...  6.53 us
    pallas_call x1, Pallas kernels, write(): pl.pallas_call(write_kernel, out_shape=jax.ShapeDtypeStruct(grad.shape, g...  2.4 us

profile of v6, /device:TPU:0, one launch (start us, length us, event | category | flops | bytes accessed | tf_op | source)
XLA Modules:
  0.0 58.9 jit_solution(6048381330578783606)
XLA Ops:
  0.6 6.5 %attention.1 = (bf16[192,1024]{1,0:T(8,128)(2,1)}, bf16[80,1024]{1,0:T(8,128)(2,1)}, bf16[80,1024]{1,0:T(8,128)(2,1)}) custom-call(s32[32]{0:T(128)} %ctx_ref.1, s32[512]{0:T(512)} %accepted_ref.1, bf16[32,48,128]{2,1,0:T(8,128)(2,1)} %bitcast.13, bf16[32,1024,128]{2,1,0:T(8,128)(2,1)} %bitcast.9, bf16[32,1024,128]{2,1,0:T(8,128)(2,1)} %bitcast.10, ...), custom_call_target="tpu_custom_call" | custom-call | tf_op jit(solution)/shard_map/attention/pallas_call | solution.py:142
  7.2 49.3 %gradient.1.in_ref = f32[512,1024]{1,0:T(8,128)} custom-call(bf16[80,1024]{1,0:T(8,128)(2,1)} %get-tuple-element.6.used_ref, bf16[80,1024]{1,0:T(8,128)(2,1)} %get-tuple-element.7.foll_ref, bf16[512,1024]{1,0:T(8,128)(2,1)} %bitcast.12), custom_call_target="tpu_custom_call" | custom-call | tf_op jit(solution)/shard_map/gradient/pallas_call | solution.py:592
  56.5 2.4 %write.1 = f32[512,1024]{1,0:T(8,128)} custom-call(f32[512,1024]{1,0:T(8,128)} %gradient.1.in_ref), custom_call_target="tpu_custom_call" | custom-call | tf_op jit(solution)/shard_map/write/pallas_call | solution.py:646
